TPU v7x, 32 devices: a whole 2x2x4 slice. The times are simulated.
32 devices in a mesh: row: 4 (over y, x), col: 8 (over z, core).
Axes of the slice: x: 2, y: 2, z: 4, core: 2. Of those that a mesh axis runs over, the one named last changes fastest.
Arguments:
- inputs: bfloat16 [1536, 8192], P('col', 'row'), may hold values from -6 to 6
- segments: int32 [8192], P('row'), may hold values from 0 to 47, never falling along the last dimension, each value on 1 to 512 neighbouring positions
- mix_gain: float32 [1536], P('col'), may hold values from 0.5 to 1.5
- branch_weight: bfloat16 [1536, 2048], P('row', 'col'), may hold values from -0.15625 to 0.15625
- recur_weight: bfloat16 [1536, 2048], P('row', 'col'), may hold values from -0.15625 to 0.15625
- kernel: float32 [4, 2048], P(None, 'col'), may hold values from -3 to 3
- offsets: float32 [2048], P('col'), may hold values from -3 to 3
- retain_weight: float32 [32, 64, 64], P('col'), may hold values from -0.75 to 0.75
- retain_bias: float32 [2048], P('col'), may hold values from -4 to 4
- admit_weight: float32 [32, 64, 64], P('col'), may hold values from -0.75 to 0.75
- admit_bias: float32 [2048], P('col'), may hold values from -4 to 4
- lambdas: float32 [2048], P('col'), may hold values from 2.3 to 7.4, as said below
- merge_weight: bfloat16 [2048, 1536], P('col', 'row'), may hold values from -0.375 to 0.375
- feed_gain: float32 [1536], P('col'), may hold values from 0.5 to 1.5
- gate_weight: bfloat16 [1536, 4608], P('row', 'col'), may hold values from -0.15625 to 0.15625
- up_weight: bfloat16 [1536, 4608], P('row', 'col'), may hold values from -0.15625 to 0.15625
- down_weight: bfloat16 [4608, 1536], P('col', 'row'), may hold values from -0.125 to 0.125
- cotangent: bfloat16 [1536, 8192], P('col', 'row'), may hold values from -6 to 6
Outputs:
- result: bfloat16 [1536, 8192], P('col', 'row')
- input_grad: float32 [1536, 8192], P('col', 'row')
- grad_mix: float32 [1536], P('col')
- grad_branch: float32 [1536, 2048], P('row', 'col')
- grad_recur: float32 [1536, 2048], P('row', 'col')
- grad_kernel: float32 [4, 2048], P(None, 'col')
- grad_offsets: float32 [2048], P('col')
- grad_retain: float32 [32, 64, 64], P('col')
- bias_retain: float32 [2048], P('col')
- grad_admit: float32 [32, 64, 64], P('col')
- bias_admit: float32 [2048], P('col')
- grad_lambdas: float32 [2048], P('col')
- grad_merge: float32 [2048, 1536], P('col', 'row')
- grad_feed: float32 [1536], P('col')
- grad_gate: float32 [1536, 4608], P('row', 'col')
- grad_up: float32 [1536, 4608], P('row', 'col')
- grad_down: float32 [4608, 1536], P('col', 'row')
Inputs may be any that keep to these rules, and one draw needn't show every extreme that they name: `segments`: segment numbers never fall along the tokens; a document has 1 to 512 tokens and one has exactly 512. 8 * softplus(-lambdas) lies between 0.005 and 0.7.
All inputs are finite; a program needn't handle non-finite values.
Results may differ from a plain program's by a relative error of at most 0.0091.
Values may be sent and summed in bfloat16 or wider, within the bound.
A program may use at most 192 MiB of HBM per device.

v0:
```python
import functools

import jax
import jax.numpy as jnp
from jax import lax
from jax.experimental import pallas as pl
from jax.experimental.pallas import tpu as pltpu
from jax.sharding import PartitionSpec as P

D = 1536
SEQ = 1024
MICRO = 2


HIGH = lax.Precision.HIGHEST
EPS = 1e-06
POWER = 8.0
FLOOR = 0.01


def combine(earlier, later):
    first_a, first_b = earlier
    second_a, second_b = later
    return (first_a * second_a, second_a * first_b + second_b)


def mixer(
    branch_pre,
    lru_pre,
    segs,
    kernel,
    offsets,
    retain_weight,
    retain_bias,
    admit_weight,
    admit_bias,
    lambdas,
):
    length = lru_pre.shape[0]
    channels = lru_pre.shape[1]
    conv = offsets + kernel[0] * lru_pre
    for lag in range(1, kernel.shape[0]):
        shifted = jnp.concatenate(
            [jnp.zeros((lag, channels), lru_pre.dtype), lru_pre[:-lag]], axis=0
        )
        prior = jnp.concatenate([jnp.full((lag,), -1, jnp.int32), segs[:-lag]])
        keep = (prior == segs).astype(lru_pre.dtype)
        conv = conv + kernel[lag] * shifted * keep[:, None]
    heads = retain_weight.shape[0]
    blocks = conv.reshape(length, heads, channels // heads)
    retain = jax.nn.sigmoid(
        jnp.einsum("thi,hij->thj", blocks, retain_weight, precision=HIGH).reshape(length, channels)
        + retain_bias
    )
    admit = jax.nn.sigmoid(
        jnp.einsum("thi,hij->thj", blocks, admit_weight, precision=HIGH).reshape(length, channels)
        + admit_bias
    )
    decay = jnp.exp(-POWER * retain * jax.nn.softplus(-lambdas))
    factor = jnp.sqrt(1.0 - decay * decay + FLOOR)
    starts = jnp.concatenate([jnp.ones((1,), bool), segs[1:] != segs[:-1]])
    decay = jnp.where(starts[:, None], 0.0, decay)
    factor = jnp.where(starts[:, None], 1.0, factor)
    _, state = lax.associative_scan(combine, (decay, factor * admit * conv), axis=0)
    return jax.nn.gelu(branch_pre) * state


def geglu(gate, upper):
    return jax.nn.gelu(gate) * upper


def contract_rows(left, right):
    return lax.dot_general(
        left, right, (((0,), (0,)), ((), ())), preferred_element_type=jnp.float32
    )


def contract_cols(left, right):
    return lax.dot_general(
        left, right, (((1,), (1,)), ((), ())), preferred_element_type=jnp.float32
    )


def contract_cross(left, right):
    return lax.dot_general(
        left, right, (((0,), (1,)), ((), ())), preferred_element_type=jnp.float32
    )


def norm_forward(resid, gain):
    total = lax.psum(jnp.sum(resid * resid, axis=0), "col")
    scale = lax.rsqrt(total / D + EPS)[None, :]
    return (scale, (resid * scale * gain[:, None]).astype(jnp.bfloat16))


def norm_backward(resid, scale, gain, grad_normed):
    weighted = grad_normed * gain[:, None]
    total = lax.psum(jnp.sum(weighted * resid, axis=0), "col")
    grad_resid = scale * weighted - resid * (scale * scale * scale) * (total / D)[None, :]
    grad_gain = jnp.sum(grad_normed * resid * scale, axis=1)
    return (grad_resid, grad_gain)


def gather_features(normed):
    return lax.all_gather(normed, "col", axis=0, tiled=True)


def gather_cotangent(grad):
    return lax.all_gather(grad, "col", axis=0, tiled=True)


def spread_sum(term):
    return lax.psum_scatter(
        term.astype(jnp.bfloat16), "col", scatter_dimension=0, tiled=True
    ).astype(jnp.float32)


def back_sum(term):
    return spread_sum(term)


def merge_term(whole_merge, mixed_low):
    return spread_sum(contract_cross(whole_merge, mixed_low))


def weight_grads(normed, grad_joined):
    return jnp.dot(
        normed,
        grad_joined,
        preferred_element_type=jnp.float32,
    )


def row_sum(total, axis):
    return lax.psum_scatter(
        total.astype(jnp.bfloat16), "row", scatter_dimension=axis, tiled=True
    ).astype(jnp.float32)


def body(
    inputs,
    segments,
    mix_gain,
    branch_weight,
    recur_weight,
    kernel,
    offsets,
    retain_weight,
    retain_bias,
    admit_weight,
    admit_bias,
    lambdas,
    merge_weight,
    feed_gain,
    gate_weight,
    up_weight,
    down_weight,
    cotangent,
):
    lru_cols = branch_weight.shape[1]
    feed_cols = gate_weight.shape[1]
    mixer_params = (kernel, offsets, retain_weight, retain_bias, admit_weight, admit_bias, lambdas)
    acc_branch = jnp.zeros((D, lru_cols), jnp.float32)
    acc_recur = jnp.zeros((D, lru_cols), jnp.float32)
    acc_gate = jnp.zeros((D, feed_cols), jnp.float32)
    acc_up = jnp.zeros((D, feed_cols), jnp.float32)
    acc_merge = jnp.zeros((lru_cols, D), jnp.float32)
    acc_down = jnp.zeros((feed_cols, D), jnp.float32)
    acc_small = tuple((jnp.zeros_like(p) for p in mixer_params))
    acc_mix = jnp.zeros_like(mix_gain)
    acc_feed = jnp.zeros_like(feed_gain)
    outputs = []
    in_grads = []
    for batch in range(MICRO):
        lower = batch * SEQ
        resid_in = inputs[:, lower : lower + SEQ].astype(jnp.float32)
        grad_out = cotangent[:, lower : lower + SEQ].astype(jnp.float32)
        segs = segments[lower : lower + SEQ]
        whole_branch, whole_recur, whole_gate, whole_up = (
            lax.all_gather(branch_weight, "row", axis=0, tiled=True),
            lax.all_gather(recur_weight, "row", axis=0, tiled=True),
            lax.all_gather(gate_weight, "row", axis=0, tiled=True),
            lax.all_gather(up_weight, "row", axis=0, tiled=True),
        )
        whole_merge, whole_down = (
            lax.all_gather(merge_weight, "row", axis=1, tiled=True),
            lax.all_gather(down_weight, "row", axis=1, tiled=True),
        )
        scale_one, normed_one = norm_forward(resid_in, mix_gain)
        full_one = gather_features(normed_one)
        branch_pre = contract_rows(full_one, whole_branch)
        lru_pre = contract_rows(full_one, whole_recur)

        def local_mixer(bpre, lpre, kern, offs, rweight, rbias, aweight, abias, lams):
            return mixer(bpre, lpre, segs, kern, offs, rweight, rbias, aweight, abias, lams)

        mixed, mixer_pull = jax.vjp(local_mixer, branch_pre, lru_pre, *mixer_params)
        mixed_low = mixed.astype(jnp.bfloat16)
        resid_mid = resid_in + merge_term(whole_merge, mixed_low)
        scale_two, normed_two = norm_forward(resid_mid, feed_gain)
        full_two = gather_features(normed_two)
        gate = contract_rows(full_two, whole_gate)
        upper = contract_rows(full_two, whole_up)
        hidden, geglu_pull = jax.vjp(geglu, gate, upper)
        hidden_low = hidden.astype(jnp.bfloat16)
        result = resid_mid + spread_sum(contract_cross(whole_down, hidden_low))
        outputs.append(result.astype(jnp.bfloat16))
        grad_full = gather_cotangent(grad_out.astype(jnp.bfloat16))
        acc_down = acc_down + contract_cross(hidden_low, grad_full)
        grad_gate, grad_upper = geglu_pull(contract_cross(grad_full, whole_down))
        grad_gate = grad_gate.astype(jnp.bfloat16)
        grad_upper = grad_upper.astype(jnp.bfloat16)
        feed_joined = weight_grads(full_two, jnp.concatenate([grad_gate, grad_upper], axis=1))
        acc_gate = acc_gate + feed_joined[:, :feed_cols]
        acc_up = acc_up + feed_joined[:, feed_cols:]
        grad_normed_two = back_sum(
            contract_cols(whole_gate, grad_gate) + contract_cols(whole_up, grad_upper)
        )
        grad_mid_norm, feed_part = norm_backward(resid_mid, scale_two, feed_gain, grad_normed_two)
        acc_feed = acc_feed + feed_part
        grad_mid = grad_out + grad_mid_norm
        grad_mid_full = gather_cotangent(grad_mid.astype(jnp.bfloat16))
        acc_merge = acc_merge + contract_cross(mixed_low, grad_mid_full)
        pulled = mixer_pull(contract_cross(grad_mid_full, whole_merge))
        grad_branch = pulled[0].astype(jnp.bfloat16)
        grad_lru = pulled[1].astype(jnp.bfloat16)
        acc_small = tuple((total + part for total, part in zip(acc_small, pulled[2:])))
        branch_joined = weight_grads(full_one, jnp.concatenate([grad_branch, grad_lru], axis=1))
        acc_branch = acc_branch + branch_joined[:, :lru_cols]
        acc_recur = acc_recur + branch_joined[:, lru_cols:]
        grad_normed_one = back_sum(
            contract_cols(whole_branch, grad_branch) + contract_cols(whole_recur, grad_lru)
        )
        grad_in_norm, mix_part = norm_backward(resid_in, scale_one, mix_gain, grad_normed_one)
        acc_mix = acc_mix + mix_part
        in_grads.append(grad_mid + grad_in_norm)
    sum_branch, sum_recur, sum_gate, sum_up = (
        row_sum(acc_branch, 0),
        row_sum(acc_recur, 0),
        row_sum(acc_gate, 0),
        row_sum(acc_up, 0),
    )
    sum_merge, sum_down = (
        row_sum(acc_merge, 1),
        row_sum(acc_down, 1),
    )
    summed = lax.psum(
        (
            acc_mix,
            acc_feed,
            acc_small[0],
            acc_small[1],
            acc_small[2],
            acc_small[3],
            acc_small[4],
            acc_small[5],
            acc_small[6],
        ),
        "row",
    )
    result_all = jnp.concatenate(outputs, axis=1)
    input_grad = jnp.concatenate(in_grads, axis=1)
    return (
        result_all,
        input_grad,
        summed[0],
        sum_branch,
        sum_recur,
        summed[2],
        summed[3],
        summed[4],
        summed[5],
        summed[6],
        summed[7],
        summed[8],
        sum_merge,
        summed[1],
        sum_gate,
        sum_up,
        sum_down,
    )


MESH = pl.DeviceIdType.MESH
F32 = jnp.float32
BF16 = jnp.bfloat16
LINE = 4
PART = 128
PARTS = 8
LATE = 256
GELU_A = 0.7978845608028654
GELU_B = 0.044715


def place():
    row, col = lax.axis_index("row"), lax.axis_index("col")
    return row, col // 2, col % 2


def at_line(z, core):
    return {"col": 2 * z + core}


def lanes(part):
    return pl.ds(pl.multiple_of(part * PART, PART), PART)


def rows_of(index, size):
    return pl.ds(pl.multiple_of(index * size, 16), size)


def dot(a, b):
    return lax.dot_general(a, b, (((1,), (0,)), ((), ())), preferred_element_type=F32)


def dot_nt(a, b):
    return lax.dot_general(a, b, (((1,), (1,)), ((), ())), preferred_element_type=F32)


def greet(row, z, core, rows, line):
    barrier = pltpu.get_barrier_semaphore()
    peers = [{"col": 2 * z + (1 - core)}]
    if rows:
        peers += [{"row": row ^ d} for d in (1, 2, 3)]
    if line:
        peers += [at_line(z ^ d, core) for d in (1, 2, 3)]
    for peer in peers:
        pl.semaphore_signal(barrier, inc=1, device_id=peer, device_id_type=MESH)
    return functools.partial(pl.semaphore_wait, barrier, len(peers))


def remote(src, dst, send, recv, peer):
    return pltpu.make_async_remote_copy(
        src_ref=src, dst_ref=dst, send_sem=send, recv_sem=recv, device_id=peer, device_id_type=MESH
    )


class Gather:
    def __init__(self, ref, send, recv, z, core, block, back=False):
        self.parts = ref.shape[0]
        self.ref, self.sems, self.z, self.core = ref, (send, recv), z, core
        self.block, self.back = block, back

    def copy(self, way, hop, step, owner, incoming=False):
        part = self.parts - 1 - step if self.back else step
        piece = self.ref.at[part, rows_of(owner, self.block), :]
        peer = at_line(self.z + (1 if (way == 0) != incoming else -1), self.core)
        return remote(piece, piece, self.sems[0].at[way, hop, step], self.sems[1].at[way, hop, step], peer)

    def each(self, hop, act, incoming):
        z = self.z
        if incoming:
            cases = ((0, z - 1 - hop >= 0, z - 1 - hop), (1, z + 1 + hop < LINE, z + 1 + hop))
        else:
            cases = (
                (0, (z >= hop) & (z < LINE - 1), z - hop),
                (1, (z + hop < LINE) & (z >= 1), z + hop),
            )
        for way, here, owner in cases:
            pl.when(here)(functools.partial(act, way, owner))

    def send(self, hop, step):
        self.each(hop, lambda way, owner: self.copy(way, hop, step, owner).start(), False)

    def arrive(self, hop, step):
        self.each(hop, lambda way, owner: self.copy(way, hop, step, owner, True).wait_recv(), True)

    def forward(self, hop, step):
        self.arrive(hop - 1, step)
        self.send(hop, step)

    def sent(self):
        def one(step, carry):
            for hop in range(LINE - 1):
                self.each(hop, lambda way, owner: self.copy(way, hop, step, owner).wait_send(), False)
            return carry

        lax.fori_loop(0, self.parts, one, 0)

    def middle(self, step, ahead=1):
        for hop in (2, 1, 0):
            later = step + ahead + 2 - hop
            act = self.forward if hop else self.send
            pl.when(later < self.parts)(functools.partial(act, hop, later))


class Spread:
    def __init__(self, own, held, send, recv, z, core):
        self.parts = held.shape[0]
        self.own, self.held, self.sems, self.z, self.core = own, held, (send, recv), z, core

    def copy(self, way, step, hop):
        slot = hop if way == 0 else LINE - hop
        there = slot - 1 if way == 0 else slot + 1
        peer = at_line(self.z + (1 if way == 0 else -1), self.core)
        return remote(
            self.held.at[step, slot],
            self.held.at[step, there],
            self.sems[0].at[way, step, hop],
            self.sems[1].at[way, step, hop - 1],
            peer,
        )

    def landed(self, way, step, hop):
        slot = hop if way == 0 else LINE - hop
        piece = self.held.at[step, slot]
        peer = at_line(self.z + (-1 if way == 0 else 1), self.core)
        remote(piece, piece, self.sems[0].at[way, step, hop], self.sems[1].at[way, step, hop], peer).wait_recv()

    def push(self, way, step, first):
        z = self.z

        def one(i, carry):
            hop = LINE - 1 - i
            owner = z + hop if way == 0 else z - hop
            slot = hop if way == 0 else LINE - hop

            @pl.when((owner >= 0) & (owner < LINE))
            def _():
                @pl.when(first)
                def _():
                    self.held[step, slot] = self.own(step, owner)[...].astype(BF16)

                @pl.when(jnp.logical_not(first))
                def _():
                    self.landed(way, step, hop)
                    total = self.own(step, owner)[...].astype(F32) + self.held[step, slot].astype(F32)
                    self.held[step, slot] = total.astype(BF16)

                self.copy(way, step, hop).start()

            return carry

        lax.fori_loop(0, LINE - 1, one, 0)

    def serve(self, t, finish):
        z = self.z
        step = t - (LINE - 1)

        @pl.when((step >= 0) & (step < self.parts))
        def _():
            @pl.when(z == 0)
            def _():
                self.landed(1, step, 0)
                finish(step, lambda a, n: self.mine(step, a, n) + self.got(step, LINE, a, n))

            @pl.when(z == LINE - 1)
            def _():
                self.landed(0, step, 0)
                finish(step, lambda a, n: self.mine(step, a, n) + self.got(step, 0, a, n))

            @pl.when((z > 0) & (z < LINE - 1))
            def _():
                self.landed(0, step, 0)
                self.landed(1, step, 0)
                finish(
                    step,
                    lambda a, n: self.mine(step, a, n) + (self.got(step, 0, a, n) + self.got(step, LINE, a, n)),
                )

        for way, late, turn in ((1, LINE - 1 - z, z < 2), (0, z, z >= 0), (1, LINE - 1 - z, z >= 2)):
            step = t - late
            pl.when((step >= 0) & (step < self.parts) & turn)(functools.partial(self.push, way, step, late == 0))

    def mine(self, step, start, size):
        return self.own(step, self.z)[pl.ds(start, size), :].astype(F32)

    def got(self, step, slot, start, size):
        return self.held[step, slot, pl.ds(start, size)].astype(F32)

    def sent(self):
        z = self.z

        def one(step, carry):
            for way in (0, 1):
                for hop in range(1, LINE):
                    owner = z + hop if way == 0 else z - hop

                    @pl.when((owner >= 0) & (owner < LINE))
                    def _():
                        self.copy(way, step, hop).wait_send()

            return carry

        lax.fori_loop(0, self.parts, one, 0)


def share_line(ref, send, recv, z, core):
    copies = [
        remote(ref.at[z], ref.at[z], send.at[d - 1], recv.at[d - 1], at_line(z ^ d, core)) for d in (1, 2, 3)
    ]
    for copy in copies:
        copy.start()
    for d in (1, 2, 3):
        piece = ref.at[z ^ d]
        remote(piece, piece, send.at[d - 1], recv.at[d - 1], at_line(z ^ d, core)).wait_recv()
    for copy in copies:
        copy.wait_send()


class Weights:
    def __init__(self, src, dst, send, recv, own, row, z, core, turned, stride=0, start=0):
        self.src, self.dst, self.send, self.recv, self.own = src, dst, send, recv, own
        self.row, self.core, self.turned = row, core, turned
        self.stride, self.first = stride or src.shape[0], start
        self.sibling = {"col": 2 * z + (1 - core)}

    def spot(self, row, core):
        down, right = (row, core) if self.turned else (core, row)
        rows, cols = self.src.shape
        at = pl.ds(pl.multiple_of(down * self.stride + self.first, 16), rows)
        return self.dst.at[at, pl.ds(pl.multiple_of(right * cols, 128), cols)]

    def to_row(self, d):
        return remote(
            self.src, self.spot(self.row, self.core), self.send.at[d], self.recv.at[d], {"row": self.row ^ d}
        )

    def to_sibling(self, d):
        if d == 0:
            return remote(
                self.src, self.spot(self.row, self.core), self.send.at[0], self.recv.at[0], self.sibling
            )
        piece = self.spot(self.row ^ d, self.core)
        return remote(piece, piece, self.send.at[3 + d], self.recv.at[3 + d], self.sibling)

    def local(self):
        return pltpu.make_async_copy(self.src, self.spot(self.row, self.core), self.own)

    def start(self):
        for d in (1, 2, 3):
            self.to_row(d).start()
        self.to_sibling(0).start()
        self.local().start()

    def forward(self):
        for d in (1, 2, 3):
            piece = self.spot(self.row ^ d, self.core)
            remote(piece, piece, self.send.at[d], self.recv.at[d], {"row": self.row ^ d}).wait_recv()
            self.to_sibling(d).start()

    def finish(self):
        self.local().wait()
        for d in (0, 1, 2, 3):
            piece = self.spot(self.row ^ d, 1 - self.core)
            sem = 0 if d == 0 else 3 + d
            remote(piece, piece, self.send.at[sem], self.recv.at[sem], self.sibling).wait_recv()

    def sent(self):
        for d in (1, 2, 3):
            self.to_row(d).wait_send()
            self.to_sibling(d).wait_send()
        self.to_sibling(0).wait_send()


def gelu_parts(b):
    t = jnp.tanh(GELU_A * (b + GELU_B * (b * b * b)))
    half = 0.5 + 0.5 * t
    slope = half + (0.5 * b) * (1.0 - t * t) * (GELU_A + (3.0 * GELU_A * GELU_B) * (b * b))
    return b * half, slope


def eight(v):
    return jnp.sum(v.reshape(v.shape[0] // 8, 8, v.shape[1]), axis=0)


def fold(v):
    total = v[:, 0:128]
    for j in range(1, v.shape[1] // 128):
        total = total + v[:, j * 128 : (j + 1) * 128]
    return total


def tokens_of(ref, piece):
    return jnp.concatenate([ref[k, piece, :] for k in range(ref.shape[0])], axis=1)


def blocks(count, body):
    def one(i, carry):
        body(i)
        return carry

    lax.fori_loop(0, count, one, 0)


def scale_of(ref, eps, width):
    total = jnp.sum(jnp.sum(ref[...], axis=0), axis=0, keepdims=True)
    return lax.rsqrt(total / width + eps)


def forward_kernel(
    width, eps,
    x_in, g_in, segs, taps, offs, bias_r, bias_a, decay, mix, late, retain, admit, branch, recur, mn_s, gu_s, d_s,
    masks, par, gains, gates, coef, scale, scale_two, y_out, n1_out, q_out, x_out, g_out, b_out, p_out, u_out, r_out, i_out, h_out,
    result, dn2_out, dev_h, z_h, g_own, g_got, gd_own, gd_got, br_n, m_n,
    sums, sums2, sums3, vec, br_s, brn_s, m_s, vec_all, block_all, gates_hi, gates_lo, normed, normed2, go, x_own, y, dn2, q_c, p_s, h_s, room, uh, ul,
    own, held, held_n, held_o, gu, gun, down, dt, zs, dev,
    x_send, x_recv, x_loc, i_send, i_recv, i_loc, l_send, l_recv, n_send, n_recv, c_send, c_recv, g_send, g_recv, e_send, e_recv, f_send, f_recv,
    s_send, s_recv, t_send, t_recv, o_send, o_recv, w_send, w_recv, w_own, k_sem, v_sem, d_send, d_recv, d_own,
):
    row, z, core = place()
    block, seq = y.shape
    half = x_in.shape[0]
    chan = p_s.shape[0]
    hid = zs.shape[0]
    b_s, u_s, r_s, i_s, a_c = [room.at[n * chan : (n + 1) * chan, :] for n in range(5)]
    ev, dz = room.at[0 : 2 * hid, :], room.at[2 * hid : 3 * hid, :]
    hh = hid // 2
    hc = chan // 2
    sibling = {"col": 2 * z + (1 - core)}
    met = greet(row, z, core, True, True)
    br_s[0:hc, :] = branch[...].T
    br_s[hc:, :] = recur[...].T
    m_s[...] = mn_s[...].T
    br, mt = gun.at[0 : 2 * chan, 0:width], dt.at[:, 0:chan]
    wide = br_s.shape[0]
    recur_s, branch_s = br_s.at[wide // 2 :, :], br_s.at[0 : wide // 2, :]
    weights = [
        Weights(src, dst, w_send.at[n], w_recv.at[n], w_own.at[n], row, z, core, n in (2, 5), stride, start)
        for n, (src, dst, stride, start) in enumerate(
            (
                (recur_s, br, hc, 0),
                (branch_s, br, hc, chan),
                (m_s, mt, 0, 0),
                (gu_s, gu, 0, 0),
                (d_s, down, 0, 0),
                (brn_s, br_n, 0, 0),
                (mn_s, m_n, 0, 0),
            )
        )
    ]
    mine = pl.ds(pl.multiple_of(core * seq, seq), seq)
    other = pl.ds(pl.multiple_of((1 - core) * seq, seq), seq)
    inner = pl.ds(pl.multiple_of(z * block + core * half, 16), half)
    outer = rows_of(core, half)
    swaps = [
        remote(x_in.at[:, other], x_own.at[outer, :], x_send.at[0], x_recv.at[0], sibling),
        pltpu.make_async_copy(x_in.at[:, mine], x_own.at[outer, :], x_loc.at[0]),
    ]
    for k in range(PARTS):
        theirs, ours = [pl.ds(pl.multiple_of(c * seq + k * PART, 128), PART) for c in (1 - core, core)]
        swaps.append(remote(g_in.at[:, theirs], go.at[k, inner, :], i_send.at[k], i_recv.at[k], sibling))
        swaps.append(pltpu.make_async_copy(g_in.at[:, ours], go.at[k, inner, :], i_loc.at[k]))
    vec[...] = jnp.zeros(vec.shape, F32)
    vec[0:4, :] = taps[...]
    for n, one_row in enumerate((offs, bias_r, bias_a)):
        vec[4 + n : 5 + n, :] = one_row[...]
    rate = -decay[...]
    vec[7:8, :] = 8.0 * (jnp.maximum(rate, 0.0) + jnp.log1p(jnp.exp(-jnp.abs(rate))))
    vec[8:9, 0:half] = mix[...]
    vec[9:10, 0:half] = late[...]
    brn_s[:, 0:hc] = branch[...]
    brn_s[:, hc:] = recur[...]
    met()
    for w in weights[:3]:
        w.start()
    for swap in swaps:
        swap.start()
    trades = []
    for n, (src, dst) in enumerate(
        ((vec, vec_all.at[core]), (retain, block_all.at[core, 0]), (admit, block_all.at[core, 1]))
    ):
        trades.append(remote(src, dst, x_send.at[2 + n], x_recv.at[2 + n], sibling))
        trades.append(pltpu.make_async_copy(src, dst, x_loc.at[2 + n]))
    for trade in trades:
        trade.start()
    for swap in swaps + trades:
        swap.wait()
    flushes = [
        pltpu.make_async_copy(x_own, x_out, v_sem.at[0]),
        pltpu.make_async_copy(go.at[:, rows_of(z, block), :], g_out, v_sem.at[1]),
    ]
    for flush in flushes:
        flush.start()
    gather = Gather(normed, g_send, g_recv, z, core, block)
    gather_go = Gather(go, e_send, e_recv, z, core, block)
    gather_two = Gather(normed2, f_send, f_recv, z, core, block)
    shares = lambda k, s: own.at[k, s]
    shares_o = lambda k, s: normed.at[k, rows_of(s, block), :]
    spread = Spread(shares, held, s_send, s_recv, z, core)
    spread_n = Spread(shares, held_n, t_send, t_recv, z, core)
    spread_o = Spread(shares_o, held_o, o_send, o_recv, z, core)
    res = x_own
    gather_go.send(0, 0)
    gather_go.send(0, 1)
    for c in (0, 1):
        at = slice(c * hc, (c + 1) * hc)
        par[at, :] = vec_all[c].T
        gains[c * half : (c + 1) * half, :] = par[c * hc : c * hc + half, :]

    sums[z] = jnp.zeros(sums.shape[1:], F32)

    def squares(i):
        v = x_own[rows_of(i, 16), :].astype(F32)
        v = v * v
        sums[z] += v[:8] + v[8:]

    blocks(block // 16, squares)
    share_line(sums, l_send, l_recv, z, core)
    scale[...] = jnp.broadcast_to(scale_of(sums, eps, width), scale.shape)

    def norm(i):
        v = x_own[rows_of(i, 16), :].astype(F32) * scale[0:1, :] * gains[rows_of(i, 16), 8:9]
        v = v.astype(BF16)
        for k in range(PARTS):
            normed[k, pl.ds(pl.multiple_of(z * block + i * 16, 16), 16), :] = v[:, k * PART : (k + 1) * PART]

    blocks(block // 16, norm)
    gather.send(0, 0)
    gather.send(0, 1)
    p_s[:, PART:] = jnp.zeros((chan, 128), F32)
    h_s[:, PART:] = jnp.zeros((chan, 128), F32)
    pads = [
        pltpu.make_async_copy(src.at[:, PART:], out.at[:, 0:128], v_sem.at[2 + n])
        for n, (src, out) in enumerate(((p_s, p_out), (h_s, h_out)))
    ]
    for pad in pads:
        pad.start()
    gates[...] = jnp.zeros(gates.shape, BF16)
    gates_hi[...] = jnp.zeros(gates_hi.shape, BF16)
    gates_lo[...] = jnp.zeros(gates_lo.shape, BF16)
    per = retain.shape[0]
    tap = retain.shape[1]
    for c in (0, 1):
        for n in (0, 1):
            for e in range(per):
                w = block_all[c, n, e]
                at, far = slice(e * tap, (e + 1) * tap), slice(n * hc + e * tap, n * hc + (e + 1) * tap)
                gates[c, at, far] = w.astype(BF16)
                w = w.T
                high = w.astype(BF16)
                gates_hi[c, far, at] = high
                gates_lo[c, far, at] = (w - high.astype(F32)).astype(BF16)
    masks[...] = jnp.zeros(masks.shape, F32)
    here = jnp.broadcast_to(segs[:, mine], (8, seq))
    spot = lax.broadcasted_iota(jnp.int32, (8, seq), 1)
    for lag in (1, 2, 3):
        same = jnp.where((pltpu.roll(here, lag, 1) == here) & (spot >= lag), 1.0, 0.0)
        masks[lag : lag + 1, 0:seq] = same[0:1]
        if lag == 1:
            masks[0:1, 0:seq] = 1.0 - same[0:1]
    gather.forward(1, 0)
    gather.send(0, 2)
    gather_go.forward(1, 0)
    gather.forward(1, 1)
    gather.forward(2, 0)
    weights[0].forward()
    gather_go.forward(1, 1)
    gather_go.forward(2, 0)
    weights[1].forward()
    for w in weights[3:5]:
        w.start()
    gather_go.forward(2, 1)
    weights[0].finish()
    for pad in pads:
        pad.wait()

    kept = (b_s, p_s, u_s, r_s, i_s, h_s, q_c)
    outs = (b_out, p_out, u_out, r_out, i_out, h_out, q_out)

    def keep(n, part):
        if n in (1, 5):
            at = pl.ds(pl.multiple_of(128 + part * PART, 128), PART)
            return pltpu.make_async_copy(kept[n].at[:, 128:], outs[n].at[:, at], k_sem.at[n])
        return pltpu.make_async_copy(kept[n], outs[n].at[:, lanes(part)], k_sem.at[n])

    def put_shares(k, whole):
        for s in range(LINE):
            own[k, s] = whole[s * block : (s + 1) * block, :].astype(own.dtype)

    def work(k):
        here = lanes(k)

        @pl.when(k > 0)
        def _():
            for n in range(len(kept)):
                keep(n, k - 1).wait()

        p_s[:, 0:128] = p_s[:, PART:]
        h_s[:, 0:128] = h_s[:, PART:]
        p_s[:, 128:] = dot(br[0:chan, :], normed[k])

        def conv(i):
            ch = rows_of(i, 64)
            window = p_s[ch, :]
            pr = par[ch, :]
            u = pr[:, 4:5] + pr[:, 0:1] * window[:, 128:]
            for lag in (1, 2, 3):
                u = u + pr[:, lag : lag + 1] * (pltpu.roll(window, lag, 1)[:, 128:] * masks[lag : lag + 1, here])
            u_s[ch, :] = u
            high = u.astype(BF16)
            uh[ch, :] = high
            ul[ch, :] = (u - high.astype(F32)).astype(BF16)

        blocks(chan // 64, conv)
        gather.middle(k)
        for g in range(chan // 256):
            at = slice(g * 256, (g + 1) * 256)
            pre = dot(gates_hi[g], uh[at, :]) + dot(gates_hi[g], ul[at, :]) + dot(gates_lo[g], uh[at, :])
            r_s[at, :] = pre[:256]
            i_s[at, :] = pre[256:]

        def gated(i):
            ch = rows_of(i, 64)
            pr = par[ch, :]
            start = masks[0:1, here] > 0.5
            r = jax.nn.sigmoid(r_s[ch, :] + pr[:, 5:6])
            gate = jax.nn.sigmoid(i_s[ch, :] + pr[:, 6:7])
            r_s[ch, :] = r
            i_s[ch, :] = gate
            a = jnp.exp(-(r * pr[:, 7:8]))
            m = jnp.where(start, 1.0, jnp.sqrt(1.0 - a * a + FLOOR))
            a_c[ch, :] = jnp.where(start, 0.0, a)
            h_s[ch, 128:] = m * gate * u_s[ch, :]

        blocks(chan // 64, gated)
        first = lax.broadcasted_iota(jnp.int32, (128, PART), 1) == 0

        def recur(i):
            ch = rows_of(i, 128)
            a, h = a_c[ch, :], h_s[ch, 128:]
            h = h + jnp.where(first, a * h_s[ch, 0:128][:, 127:128], 0.0)
            a = jnp.where(first, 0.0, a)
            shift = 1
            while shift < PART:
                h = h + a * pltpu.roll(h, shift, 1)
                if shift * 2 < PART:
                    a = a * pltpu.roll(a, shift, 1)
                shift *= 2
            h_s[ch, 128:] = h

        blocks(chan // 128, recur)

        @pl.when(k == 0)
        def _():
            weights[2].forward()
            weights[1].finish()

        b_s[...] = dot(br[chan : 2 * chan, :], normed[k])

        def mixed(i):
            ch = rows_of(i, 64)
            b = b_s[ch, :]
            t = jnp.tanh(GELU_A * (b + GELU_B * (b * b * b)))
            q_c[ch, :] = (b * (0.5 + 0.5 * t) * h_s[ch, 128:]).astype(BF16)

        blocks(chan // 64, mixed)
        pl.when(k == 0)(weights[2].finish)
        put_shares(k, dot(mt[...], q_c[...]))
        for n in range(len(kept)):
            keep(n, k).start()

    def finish(k, total):
        def add(i):
            at = pl.multiple_of(i * 64, 64)
            y[pl.ds(at, 64), lanes(k)] = x_own[pl.ds(at, 64), lanes(k)].astype(F32) + total(at, 64)

        blocks(block // 64, add)

    def square(k):
        sums2[k, z] = jnp.zeros(sums2.shape[2:], F32)

        def one(i):
            v = y[rows_of(i, 64), lanes(k)]
            sums2[k, z] += eight(v * v)

        blocks(block // 64, one)
        for d in (1, 2, 3):
            share(k, d).start()

    def share(k, d):
        return remote(
            sums2.at[k, z], sums2.at[k, z], n_send.at[k, d - 1], n_recv.at[k, d - 1], at_line(z ^ d, core)
        )

    def norm_two(k):
        for d in (1, 2, 3):
            piece = sums2.at[k, z ^ d]
            remote(piece, piece, n_send.at[k, d - 1], n_recv.at[k, d - 1], at_line(z ^ d, core)).wait_recv()
        s2 = scale_of(sums2.at[k], eps, width)
        scale_two[:, lanes(k)] = jnp.broadcast_to(s2, (8, PART))

        def one(i):
            at = rows_of(i, 64)
            v = y[at, lanes(k)] * scale_two[0:1, lanes(k)] * gains[at, 9:10]
            normed2[k, pl.ds(pl.multiple_of(z * block + i * 64, 64), 64), :] = v.astype(BF16)

        blocks(block // 64, one)

    def turn_down(i):
        at = pl.ds(pl.multiple_of(i * 128, 128), 128)
        dt[:, at] = down[at, :].T

    def turn_up(i):
        at = pl.ds(pl.multiple_of(i * 128, 128), 128)
        gun[:, at] = gu[at, :].T

    def step(t, carry):
        gather.arrive(2, t)
        work(t)
        spread.serve(t, finish)
        pl.when(t >= 3)(lambda: square(t - 3))
        pl.when(t >= 4)(lambda: norm_two(t - 4))
        pl.when((t >= 4) & (t < 7))(lambda: gather_two.send(0, t - 4))
        pl.when((t >= 6) & (t < 8))(lambda: gather_two.forward(1, t - 6))
        pl.when(t == 5)(weights[3].forward)
        return carry

    lax.fori_loop(0, PARTS, step, 0)
    for w in weights[:3]:
        w.sent()
    for w in weights[5:]:
        w.start()
    for n in range(len(kept)):
        keep(n, PARTS - 1).wait()
    flush_n = pltpu.make_async_copy(normed, n1_out, v_sem.at[4])
    flush_n.start()
    gather_go.send(0, 2)
    gather_go.send(0, 3)
    spread.serve(PARTS, finish)
    square(PARTS - 3)
    norm_two(PARTS - 4)
    gather_two.forward(2, 0)
    weights[4].forward()
    spread.serve(PARTS + 1, finish)
    square(PARTS - 2)
    norm_two(PARTS - 3)
    gather_go.forward(1, 2)
    weights[4].finish()
    blocks(hid // 128, turn_down)
    spread.serve(PARTS + 2, finish)
    square(PARTS - 1)
    norm_two(PARTS - 2)
    gather.sent()
    for flush in flushes + [flush_n]:
        flush.wait()
    weights[3].finish()
    blocks(2 * hid // 128, turn_up)
    norm_two(PARTS - 1)

    def keep_dev(k):
        return pltpu.make_async_copy(dev, dev_h.at[:, lanes(k)], v_sem.at[5])

    def keep_z(k):
        return pltpu.make_async_copy(zs, z_h.at[:, lanes(k)], v_sem.at[6])

    def feed(k):

        @pl.when(k > 0)
        def _():
            keep_dev(k - 1).wait()
            keep_z(k - 1).wait()

        ev[...] = dot(gu[...], normed2[k])
        gather_two.middle(k)
        gather_go.middle(k, 2)
        gather_go.arrive(2, k)
        dz[...] = dot(down[...], go[k])
        for c in range(2):

            def one(i):
                off = pl.multiple_of(i * 64, 64)
                e = ev[pl.ds(c * 2 * hh + off, 64), :]
                v = ev[pl.ds(c * 2 * hh + hh + off, 64), :]
                d = dz[pl.ds(c * hh + off, 64), :]
                act, slope = gelu_parts(e)
                zs[pl.ds(c * hh + off, 64), :] = (act * v).astype(BF16)
                dev[pl.ds(c * 2 * hh + off, 64), :] = (d * v * slope).astype(BF16)
                dev[pl.ds(c * 2 * hh + hh + off, 64), :] = (d * act).astype(BF16)

            blocks(hh // 64, one)
        put_shares(k, dot(gun[...], dev[...]))
        spread_n.serve(k, finish_n)
        normed[k] = dot(dt[...], zs[...]).astype(BF16)
        spread_o.serve(k, finish_o)
        keep_dev(k).start()
        keep_z(k).start()

    def finish_o(k, total):
        def add(i):
            at = pl.multiple_of(i * 64, 64)
            res[pl.ds(at, 64), lanes(k)] = (y[pl.ds(at, 64), lanes(k)] + total(at, 64)).astype(BF16)

        blocks(block // 64, add)

    def keep_n(k):
        return pltpu.make_async_copy(dn2, dn2_out.at[:, lanes(k)], v_sem.at[3])

    def finish_n(k, total):
        @pl.when(k > 0)
        def _():
            keep_n(k - 1).wait()

        sums3[k, z] = jnp.zeros(sums3.shape[2:], F32)

        def add(i):
            at = pl.multiple_of(i * 64, 64)
            d = total(at, 64)
            dn2[pl.ds(at, 64), :] = d
            sums3[k, z] += eight(d * y[pl.ds(at, 64), lanes(k)] * gains[pl.ds(at, 64), 9:10])

        blocks(block // 64, add)
        keep_n(k).start()
        for d in (1, 2, 3):
            share_c(k, d).start()

    def share_c(k, d):
        return remote(
            sums3.at[k, z], sums3.at[k, z], c_send.at[k, d - 1], c_recv.at[k, d - 1], at_line(z ^ d, core)
        )

    def feed_step(t, carry):
        gather_two.arrive(2, t)
        feed(t)
        pl.when(t == 4)(weights[5].forward)
        pl.when(t == 6)(weights[6].forward)
        return carry

    lax.fori_loop(0, PARTS, feed_step, 0)
    for w in weights[3:5]:
        w.sent()
    keep_dev(PARTS - 1).wait()
    keep_z(PARTS - 1).wait()
    dev_all, z_all = gu.at[:, 0:seq], dt.at[0:hid, 0:seq]
    loads = [pltpu.make_async_copy(dev_h, dev_all, v_sem.at[5]), pltpu.make_async_copy(z_h, z_all, v_sem.at[6])]
    for load in loads:
        load.start()
    for load in loads:
        load.wait()

    def columns(start):
        return pl.ds(pl.multiple_of(start, 128), block)

    def place_up(j):
        side = jnp.where(j >= 3, core, 1 - core)
        return side * hid + (j % 3) * block, columns((j % 3) * block)

    def send_up(j):
        at, to = place_up(j)
        return remote(gun.at[:, columns(at)], g_got.at[:, to], d_send.at[j], d_recv.at[j], sibling)

    def keep_up(j):
        at, to = place_up(j)
        return pltpu.make_async_copy(gun.at[:, columns(at)], g_own.at[:, to], d_own.at[j - 3])

    def send_down():
        return remote(down.at[rows_of(1 - core, hh), :], gd_got, d_send.at[3], d_recv.at[3], sibling)

    def keep_down():
        return pltpu.make_async_copy(down.at[rows_of(core, hh), :], gd_own, d_own.at[3])

    def grad_up(j):
        at = place_up(j)[0]
        right = pl.ds(pl.multiple_of(at, 16), block)
        for low in (0, width // 2):
            piece = slice(low, low + width // 2)
            gun[piece, columns(at)] = dot_nt(tokens_of(normed2, piece), dev_all[right, :]).astype(BF16)

        @pl.when(j < 3)
        def _():
            send_up(j).start()

        @pl.when(j >= 3)
        def _():
            keep_up(j).start()

    def grad_down(side):
        at = rows_of(side, hh)
        for low in range(0, width, 2 * block):
            piece = slice(low, low + 2 * block)
            down[at, piece] = dot_nt(z_all[at, :], tokens_of(go, piece)).astype(BF16)

    def drain(i, carry):
        t = PARTS + i
        blocks(2, lambda j: grad_up(2 * i + j))
        spread_n.serve(t, finish_n)
        spread_o.serve(t, finish_o)

        @pl.when(i < 2)
        def _():
            grad_down(jnp.where(i == 0, 1 - core, core))

        pl.when(i == 0)(lambda: send_down().start())
        pl.when(i == 1)(lambda: keep_down().start())
        return carry

    lax.fori_loop(0, LINE - 1, drain, 0)
    last = [
        remote(res.at[rows_of(1 - core, half), :], result.at[:, mine], x_send.at[0], x_recv.at[0], sibling),
        pltpu.make_async_copy(res.at[rows_of(core, half), :], result.at[:, mine], x_loc.at[0]),
        pltpu.make_async_copy(y, y_out, v_sem.at[2]),
        keep_n(PARTS - 1),
    ]
    for copy in last[:3]:
        copy.start()
    for w in weights[5:]:
        w.finish()
        w.sent()
    for one in (gather_go, gather_two, spread, spread_n, spread_o):
        one.sent()
    for k in range(PARTS):
        for d in (1, 2, 3):
            share(k, d).wait_send()
            share_c(k, d).wait_send()
            piece = sums3.at[k, z ^ d]
            remote(piece, piece, c_send.at[k, d - 1], c_recv.at[k, d - 1], at_line(z ^ d, core)).wait_recv()
        total = jnp.sum(jnp.sum(sums3[k], axis=0), axis=0, keepdims=True)
        at = slice(k * PART, (k + 1) * PART)
        s2 = scale_two[:, at]
        coef[:, at] = s2 * s2 * s2 * (total / width)
    for j in range(3):
        keep_up(j + 3).wait()
        send_up(j).wait()
    keep_down().wait()
    send_down().wait()
    for copy in last:
        copy.wait()


def back_kernel(
    width,
    y, dn2_h, g_h, x_own, scale_two, scale_one, coef_two, gains, masks, par, gates_t, m_h, br_h,
    b_h, p_h, u_h, r_h, i_h, h_h, q_h, n1_h, f_own, f_got, fd_own, fd_got,
    input_grad, tiny_v, tiny_g, f_sum, f_land, fd_sum, fd_land, g_sum, g_land, gm_sum, gm_land,
    sums, coef, m_n, br_n, b_s, p_s, u_s, r_s, i_s, h_s, dyf, dbp, dy, dn1, dq, du, dri, a_c, l_c, carry_s, own, held,
    qv, n1, f_a, f_b, fd_a, fd_b, feed_part, mix_part, small, gate_grad, g_s, g_got, gm_got,
    vec, vec_in, vec_all, gd, gd_in, gd_all,
    c_sem, k_sem, l_send, l_recv, g_send, g_recv, s_send, s_recv, r_send, r_recv,
    f_sem, f_send, f_recv, d_send, d_recv, d_own, q_send, q_recv, n_send, n_recv, v_send, v_recv,
):
    row, z, core = place()
    block, seq = y.shape
    PART, PARTS = LATE, seq // LATE

    def lanes(part):
        return pl.ds(pl.multiple_of(part * PART, PART), PART)

    half = block // 2
    chan = b_s.shape[1]
    hc = chan // 2
    sibling = {"col": 2 * z + (1 - core)}
    met = greet(row, z, core, True, True)
    load_g = pltpu.make_async_copy(g_h, g_s, c_sem.at[0])
    load_g.start()
    dn2 = dn1
    load_d = pltpu.make_async_copy(dn2_h, dn2, c_sem.at[5])
    load_d.start()
    load_m = pltpu.make_async_copy(m_h, m_n, c_sem.at[1])
    load_m.start()
    load_b = pltpu.make_async_copy(br_h, br_n, c_sem.at[2])
    load_b.start()
    load_q = pltpu.make_async_copy(q_h, qv, c_sem.at[3])
    load_n = pltpu.make_async_copy(n1_h, n1, c_sem.at[4])
    kept = (b_s, p_s, u_s, r_s, i_s, h_s)
    srcs = (b_h, p_h, u_h, r_h, i_h, h_h)

    def fetch(n, part):
        if kept[n] is p_s or kept[n] is h_s:
            at = pl.ds(pl.multiple_of(part * PART, 128), PART + 128)
        else:
            at = lanes(part)
        return pltpu.make_async_copy(srcs[n].at[:, at], kept[n].at[part % 2], k_sem.at[n, part % 2])

    def fetch_all(part):
        for n in range(len(kept)):
            fetch(n, part).start()

    fetch_all(PARTS - 1)
    load_q.start()
    load_n.start()
    du[:, 0:128] = jnp.zeros((chan, 128), F32)
    carry_s[...] = jnp.zeros(carry_s.shape, F32)
    small[...] = jnp.zeros(small.shape, F32)
    gate_grad[...] = jnp.zeros(gate_grad.shape, F32)

    load_d.wait()
    load_g.wait()
    gather = Gather(dyf, g_send, g_recv, z, core, block, back=True)

    def outer(part):
        here = slice(part * PART, (part + 1) * PART)

        def one(i):
            at = rows_of(i, 64)
            s2 = scale_two[0:1, here]
            d, v = dn2[at, here], y[at, here]
            w = fold(d * v * s2)
            feed_part[at, :] = w if part == PARTS - 1 else feed_part[at, :] + w
            few = PART // g_s.shape[2]
            g = jnp.concatenate([g_s[part * few + j, at, :] for j in range(few)], axis=1)
            v = g.astype(F32) + (s2 * (gains[at, 9:10] * d) - v * coef_two[0:1, here])
            dy[at, here] = v
            dyf[part, pl.ds(pl.multiple_of(z * block + i * 64, 64), 64), :] = v.astype(BF16)

        blocks(block // 64, one)

    outer(PARTS - 1)
    met()
    gather.send(0, 0)
    outer(PARTS - 2)
    gather.send(0, 1)
    outer(PARTS - 3)
    gather.forward(1, 0)
    gather.send(0, 2)
    for part in range(PARTS - 3):
        outer(part)
    gather.forward(1, 1)
    gather.forward(2, 0)
    spread = Spread(lambda k, s: own.at[k, s], held, s_send, s_recv, z, core)
    load_m.wait()
    load_b.wait()
    final = lax.broadcasted_iota(jnp.int32, (128, PART), 1) == PART - 1

    f_arrays = ((f_own, f_got, f_a, f_b, f_sum, f_land), (fd_own, fd_got, fd_a, fd_b, fd_sum, fd_land))

    def f_loads(d):
        pulls = []
        for n, (ours, theirs, a, b, _, _) in enumerate(f_arrays):
            if n == 0:
                piece = (rows_of(row ^ d, block), slice(None))
            else:
                piece = (slice(None), pl.ds(pl.multiple_of((row ^ d) * block, 128), block))
            pulls.append(pltpu.make_async_copy(ours.at[piece], a.at[d], f_sem.at[n, 0]))
            pulls.append(pltpu.make_async_copy(theirs.at[piece], b, f_sem.at[n, 1]))
        return pulls

    def f_out(d):
        outs = []
        for n, (_, _, a, _, kept_at, land) in enumerate(f_arrays):
            if d == 0:
                outs.append(pltpu.make_async_copy(a.at[0], kept_at, f_send.at[n, 0]))
            else:
                outs.append(
                    remote(a.at[d], land.at[d - 1], f_send.at[n, d], f_recv.at[n, d], {"row": row ^ d})
                )
        return outs

    def f_part(d):
        for pull in f_loads(d):
            pull.wait()
        for _, _, a, b, _, _ in f_arrays:

            def add(i):
                at = rows_of(i, 64)
                a[d, at, :] = (a[d, at, :].astype(F32) + b[at, :].astype(F32)).astype(BF16)

            blocks(b.shape[0] // 64, add)
        for out in f_out(d):
            out.start()
        if d > 0:
            for pull in f_loads(d - 1):
                pull.start()

    def f_step(t):
        for d in range(LINE):
            pl.when(t == LINE - 1 - d)(functools.partial(f_part, d))

    for pull in f_loads(LINE - 1):
        pull.start()

    lru = hc

    def send_m():
        return remote(m_n.at[rows_of(1 - core, lru), :], gm_got, d_send.at[1], d_recv.at[1], sibling)

    def work(t):
        k = PARTS - 1 - t
        here = lanes(k)
        wide = pl.ds(pl.multiple_of(k * PART, 128), PART + 128)
        slot = k % 2
        for n in range(len(kept)):
            fetch(n, k).wait()

        @pl.when(k > 0)
        def _():
            fetch_all(k - 1)

        dq[...] = dot(m_n[...], dyf[k])

        @pl.when(t == PARTS - 1)
        def _():
            load_q.wait()
            for low in range(0, width, 2 * block):
                piece = slice(low, low + 2 * block)
                m_n[:, piece] = dot_nt(qv[...], tokens_of(dyf, piece)).astype(BF16)
            send_m().start()

        def before(i):
            ch = rows_of(i, 64)
            c = i // (hc // 64)
            low = pl.ds(pl.multiple_of(c * hc + i * 64, 64), 64)
            pr = par[ch, :]
            d = dq[ch, :]
            act, slope = gelu_parts(b_s[slot, ch, :])
            dbp[low, here] = (d * h_s[slot, ch, :][:, 128:] * slope).astype(BF16)
            l_c[ch, :] = d * act
            a_c[ch, :] = jnp.exp(-(r_s[slot, ch, :] * pr[:, 7:8]))

        blocks(chan // 64, before)
        gather.middle(t)

        def recur(i):
            ch = rows_of(i, 128)
            start = masks[0:1, here] > 0.5
            a, lam = jnp.where(start, 0.0, a_c[ch, :]), l_c[ch, :]
            lam = lam + jnp.where(final, carry_s[ch, :][:, 0:1], 0.0)
            w = jnp.where(final, 0.0, pltpu.roll(a, PART - 1, 1))
            shift = 1
            while shift < PART:
                lam = lam + w * pltpu.roll(lam, PART - shift, 1)
                if shift * 2 < PART:
                    w = w * pltpu.roll(w, PART - shift, 1)
                shift *= 2
            carry_s[ch, :] = jnp.broadcast_to((a * lam)[:, 0:1], (128, 128))
            l_c[ch, :] = lam

        blocks(chan // 128, recur)
        f_step(t)

        def after(i):
            ch = rows_of(i, 64)
            du[ch, PART:] = du[ch, 0:128]
            pr = par[ch, :]
            start = masks[0:1, here] > 0.5
            lam, a0 = l_c[ch, :], a_c[ch, :]
            earlier = pltpu.roll(h_s[slot, ch, :], 1, 1)[:, 128:]
            r, gate, u = r_s[slot, ch, :], i_s[slot, ch, :], u_s[slot, ch, :]
            m0 = jnp.sqrt(1.0 - a0 * a0 + FLOOR)
            m = jnp.where(start, 1.0, m0)
            lm = lam * m
            lu = lam * u
            du[ch, 0:PART] = lm * gate
            da = jnp.where(start, 0.0, lam * earlier - (lu * gate) * (a0 / m0)) * a0
            dr = da * (-pr[:, 7:8]) * (r * (1.0 - r))
            di = lu * m * (gate * (1.0 - gate))
            g, o = i // 4, (i % 4) * 64
            dri[pl.ds(pl.multiple_of(g * 512 + o, 64), 64), :] = dr.astype(BF16)
            dri[pl.ds(pl.multiple_of(g * 512 + 256 + o, 64), 64), :] = di.astype(BF16)
            small[5, ch, :] += fold(dr)
            small[6, ch, :] += fold(di)
            small[7, ch, :] += fold(da * r)

        blocks(chan // 64, after)
        for g in range(chan // 256):
            at = slice(g * 256, (g + 1) * 256)
            dd = dri[g * 512 : (g + 1) * 512, :]
            du[at, 0:PART] += dot(gates_t[g], dd)
            gate_grad[g] += dot_nt(u_s[slot, at, :].astype(BF16), dd)

        def conv(i):
            ch = rows_of(i, 64)
            c = i // (hc // 64)
            low = pl.ds(pl.multiple_of((c + 1) * hc + i * 64, 64), 64)
            pr = par[ch, :]
            follow = du[ch, :]
            window = p_s[slot, ch, :]
            d = follow[:, :PART]
            dp = pr[:, 0:1] * d
            small[4, ch, :] += fold(d)
            small[0, ch, :] += fold(d * window[:, 128:])
            for lag in (1, 2, 3):
                kd = follow * masks[lag : lag + 1, wide]
                dp = dp + pr[:, lag : lag + 1] * pltpu.roll(kd, PART + 128 - lag, 1)[:, :PART]
                small[lag, ch, :] += fold(kd[:, :PART] * pltpu.roll(window, lag, 1)[:, 128:])
            dbp[low, here] = dp.astype(BF16)

        blocks(chan // 64, conv)
        whole = dot(br_n[...], dbp[:, here])
        for s in range(LINE):
            own[t, s] = whole[s * block : (s + 1) * block, :].astype(own.dtype)

    def finish(t, total):
        k = PARTS - 1 - t

        sums[k, z] = jnp.zeros(sums.shape[2:], F32)

        @pl.when(t == 0)
        def _():
            mix_part[...] = jnp.zeros(mix_part.shape, F32)

        def add(i):
            at = pl.ds(pl.multiple_of(i * 64, 64), 64)
            d = total(pl.multiple_of(i * 64, 64), 64)
            dn1[at, lanes(k)] = d
            w = d * x_own[at, lanes(k)].astype(F32)
            sums[k, z] += eight(w * gains[at, 8:9])
            w = w * scale_one[0:1, lanes(k)]
            mix_part[at, :] += fold(w)

        blocks(block // 64, add)
        for d in (1, 2, 3):
            share(k, d).start()

    def share(k, d):
        return remote(sums.at[k, z], sums.at[k, z], l_send.at[k, d - 1], l_recv.at[k, d - 1], at_line(z ^ d, core))

    def step(t, carry):
        gather.arrive(2, t)
        work(t)
        spread.serve(t, finish)
        return carry

    lax.fori_loop(0, PARTS, step, 0)
    load_n.wait()


    def cols_of(side):
        return pl.ds(pl.multiple_of(side * 2 * lru, 128), 2 * lru)

    def send_br():
        return remote(br_n.at[:, cols_of(1 - core)], g_got, d_send.at[0], d_recv.at[0], sibling)

    def grad_br(side):
        for low in range(0, width, 2 * block):
            piece = slice(low, low + 2 * block)
            br_n[piece, cols_of(side)] = dot_nt(tokens_of(n1, piece), dbp[rows_of(side, 2 * lru), :]).astype(BF16)

    def out_br(d):
        piece = br_n.at[rows_of(row ^ d, block), cols_of(core)]
        if d == 0:
            return pltpu.make_async_copy(piece, g_sum, d_own.at[0])
        return remote(piece, g_land.at[d - 1], q_send.at[0, d - 1], q_recv.at[0, d - 1], {"row": row ^ d})

    def out_m(d):
        piece = m_n.at[rows_of(core, lru), pl.ds(pl.multiple_of((row ^ d) * block, 128), block)]
        if d == 0:
            return pltpu.make_async_copy(piece, gm_sum, d_own.at[1])
        return remote(piece, gm_land.at[d - 1], q_send.at[1, d - 1], q_recv.at[1, d - 1], {"row": row ^ d})

    def drain(i, carry):
        t = PARTS + i

        @pl.when(i == 0)
        def _():
            grad_br(1 - core)
            send_br().start()
            send_m().wait_recv()

            def add(j):
                at = rows_of(j, 64)
                to = pl.ds(pl.multiple_of(core * lru + j * 64, 64), 64)
                m_n[to, :] = (m_n[to, :].astype(F32) + gm_got[at, :].astype(F32)).astype(BF16)

            blocks(lru // 64, add)
            for d in (3, 2, 1, 0):
                out_m(d).start()
            grad_br(core)

        @pl.when(i == 1)
        def _():
            send_br().wait_recv()

            def add(j):
                at = rows_of(j, 64)
                br_n[at, cols_of(core)] = (br_n[at, cols_of(core)].astype(F32) + g_got[at, :].astype(F32)).astype(BF16)

            blocks(width // 64, add)
            for d in (3, 2, 1, 0):
                out_br(d).start()
        spread.serve(t, finish)
        return carry

    lax.fori_loop(0, LINE - 1, drain, 0)
    mine = pl.ds(pl.multiple_of(core * seq, seq), seq)
    for side in (0, 1):
        for e in range(4):
            at = slice(e * 64, (e + 1) * 64)
            gd[side, at, 0:64] = gate_grad[side, at, e * 64 : (e + 1) * 64]
            gd[side, at, 64:128] = gate_grad[side, at, 256 + e * 64 : 256 + (e + 1) * 64]
    swap_gd = remote(gd.at[1 - core], gd_in, v_send.at[0], v_recv.at[0], sibling)
    swap_gd.start()
    lane = lax.broadcasted_iota(jnp.int32, (64, 128), 1)

    def columns(parts, at):
        total = jnp.zeros((64, 128), F32)
        for n, part in enumerate(parts):
            total = total + jnp.where(lane == n, jnp.sum(part(at), axis=1, keepdims=True), 0.0)
        return total

    vec[...] = jnp.zeros(vec.shape, F32)
    for j in range(chan // 64):
        at = slice(j * 64, (j + 1) * 64)
        v = columns([lambda at, n=n: small[n, at, :] for n in range(8)], at)
        vec[0, :, at] = v.T[0:8, :]

    for k in range(PARTS):
        for d in (1, 2, 3):
            share(k, d).wait_send()
            piece = sums.at[k, z ^ d]
            remote(piece, piece, l_send.at[k, d - 1], l_recv.at[k, d - 1], at_line(z ^ d, core)).wait_recv()
        total = jnp.sum(jnp.sum(sums[k], axis=0), axis=0, keepdims=True)
        at = slice(k * PART, (k + 1) * PART)
        s1 = scale_one[:, at]
        coef[:, at] = s1 * s1 * s1 * (total / width)

    def last(i):
        at = rows_of(i, 16)
        v = dy[at, :] + (
            scale_one[0:1, :] * (gains[at, 8:9] * dn1[at, :]) - x_own[at, :].astype(F32) * coef[0:1, :]
        )
        dy[at, :] = v

    blocks(block // 16, last)
    back = remote(dy.at[rows_of(1 - core, half), :], input_grad.at[:, mine], r_send, r_recv, sibling)
    back.start()
    keep_in = pltpu.make_async_copy(dy.at[rows_of(core, half), :], input_grad.at[:, mine], d_own.at[3])
    keep_in.start()
    for j in range(block // 64):
        at = slice(j * 64, (j + 1) * 64)
        v = columns([lambda at: mix_part[at, :], lambda at: feed_part[at, :]], at)
        vec[1, :, at] = v.T[0:8, :]
    swap_vec = remote(vec, vec_in, v_send.at[1], v_recv.at[1], sibling)
    swap_vec.start()
    swap_gd.wait()
    gd_all[0] = gd[core] + gd_in[...]
    rows_gd = [
        remote(gd_all.at[0], gd_all.at[d], n_send.at[0, d - 1], n_recv.at[0, d - 1], {"row": row ^ d}) for d in (1, 2, 3)
    ]
    for copy in rows_gd:
        copy.start()
    swap_vec.wait()
    vec_all[0] = vec[...] + vec_in[...]
    rows_vec = [
        remote(vec_all.at[0], vec_all.at[d], n_send.at[1, d - 1], n_recv.at[1, d - 1], {"row": row ^ d}) for d in (1, 2, 3)
    ]
    for copy in rows_vec:
        copy.start()
    spread.sent()
    gather.sent()
    for copy in rows_gd + rows_vec:
        copy.wait()
    for every, out in ((gd_all, tiny_g), (vec_all, tiny_v)):
        first, second = every[row % 2], every[1 - row % 2]
        third, fourth = every[2 + row % 2], every[3 - row % 2]
        out[...] = (first + second) + (third + fourth)
    for d in range(LINE):
        for out in f_out(d):
            out.wait()
    send_br().wait_send()
    send_m().wait_send()
    for d in (0, 1, 2, 3):
        out_br(d).wait()
        out_m(d).wait()
    for copy in (keep_in, back):
        copy.wait()


def last_kernel(
    f_sum, f_land, fd_sum, fd_land, g_sum, g_land, gm_sum, gm_land, result_in, grad_in, tiny_v, tiny_g, lambdas,
    s_b, s_r, s_m, s_g, s_u, s_d, result, input_grad, taps, offs, bias_r, bias_a, decay, mix, feed, retain, admit,
):
    lru, ff, half = s_b.shape[1], s_g.shape[0], mix.shape[1]

    def four(first, others):
        return first[...].astype(F32) + others[0].astype(F32) + (others[1].astype(F32) + others[2].astype(F32))

    v = four(f_sum, f_land)
    s_g[...] = v.T[:ff, :]
    s_u[...] = v.T[ff:, :]
    v = four(g_sum, g_land)
    s_b[...] = v[:, :lru]
    s_r[...] = v[:, lru:]
    s_d[...] = four(fd_sum, fd_land)
    result[...] = result_in[...]
    input_grad[...] = grad_in[...]

    @pl.when(pl.program_id(0) == 0)
    def _():
        core = place()[2]
        s_m[...] = four(gm_sum, gm_land)
        small = tiny_v[0, :, pl.ds(pl.multiple_of(core * lru, 128), lru)]
        taps[...] = small[0:4]
        offs[...] = small[4:5]
        bias_r[...] = small[5:6]
        bias_a[...] = small[6:7]
        decay[...] = small[7:8] * (8.0 * jax.nn.sigmoid(-lambdas[...]))
        gains = jnp.where(core == 0, tiny_v[1, :, 0:half], tiny_v[1, :, half : 2 * half])
        mix[...] = gains[0:1]
        feed[...] = gains[1:2]
        for e in range(retain.shape[0]):
            at = slice(e * 64, (e + 1) * 64)
            retain[e] = tiny_g[at, 0:64]
            admit[e] = tiny_g[at, 64:128]


ANY = pl.BlockSpec(memory_space=pl.ANY)
VM = pl.BlockSpec(memory_space=pltpu.VMEM)
DMA = pltpu.SemaphoreType.DMA
ROOM = 62 * 1024 * 1024


def shape(dims, kind):
    return jax.ShapeDtypeStruct(dims, kind)


def call(kernel, ins, outs, scratch, ident, name, flops):
    return pl.pallas_call(
        kernel,
        out_shape=[o[0] for o in outs],
        in_specs=ins,
        out_specs=[o[1] for o in outs],
        scratch_shapes=scratch,
        name=name,
        compiler_params=pltpu.CompilerParams(
            collective_id=ident, has_side_effects=True, vmem_limit_bytes=ROOM
        ),
        cost_estimate=pl.CostEstimate(flops=flops, bytes_accessed=40000000, transcendentals=0),
    )


def fast_body(
    inputs, segments, mix_gain, branch_weight, recur_weight, kernel, offsets, retain_weight, retain_bias,
    admit_weight, admit_bias, lambdas, merge_weight, feed_gain, gate_weight, up_weight, down_weight, cotangent,
):
    half, tokens = inputs.shape
    block, seq, width = 2 * half, tokens // 2, D
    lru, heads = branch_weight.shape[1], retain_weight.shape[0]
    chan = 2 * lru
    ff = gate_weight.shape[1]
    hid = 2 * ff
    rows = branch_weight.shape[0]
    cols = merge_weight.shape[1]
    gu_s = jnp.concatenate([gate_weight, up_weight], axis=1).T

    f_tok = lambda n, kind=F32: shape((n, seq), kind)
    padded = (shape((chan, 128 + seq), F32), ANY)
    state = [(f_tok(chan), ANY), padded, *[(f_tok(chan), ANY)] * 3, padded]
    line = [DMA((3,)), DMA((3,))]
    steps = [DMA((2, 3, PARTS)), DMA((2, 3, PARTS))]
    sums = [DMA((2, PARTS, LINE)), DMA((2, PARTS, LINE))]
    held = pltpu.VMEM((PARTS, LINE + 1, block, PART), BF16)
    own_low = pltpu.VMEM((PARTS, LINE, block, PART), BF16)
    tok = lambda n, kind=F32, lead=0: pltpu.VMEM((n, lead + seq), kind)
    one = lambda n, kind=F32, lead=0: pltpu.VMEM((n, lead + PART), kind)
    grad_gu, grad_d = (shape((width, 2 * ff), BF16), ANY), (shape((ff, width), BF16), ANY)
    low = lambda n, m: (shape((n, m), BF16), ANY)
    parted = lambda n: (shape((PARTS, n, PART), BF16), ANY)
    by_part = lambda n: pltpu.VMEM((PARTS, n, PART), BF16)

    (masks, par, gains, gates, coef, scale_one, scale_two, y, n1, q, x_own, g, b, p, u, r, i, h, result, dn2, _, _, f_own, f_got, fd_own, fd_got,
     br_n, m_n) = call(
        functools.partial(forward_kernel, width, EPS),
        [ANY] * 2 + [VM] * 13 + [ANY] * 2,
        [(shape((8, seq + 128), F32), VM), (shape((chan, 16), F32), VM), (shape((block, 16), F32), VM), (shape((2, lru, 2 * lru), BF16), VM),
         (f_tok(8), VM), (f_tok(8), VM), (f_tok(8), VM), (f_tok(block), ANY), parted(width), low(chan, seq), low(block, seq), parted(block)]
        + state + [low(half, tokens), (f_tok(block), ANY), low(2 * hid, seq), low(hid, seq), grad_gu, grad_gu, grad_d, grad_d,
                   low(width, 2 * chan), low(chan, width)],
        [pltpu.VMEM((LINE, 8, seq), F32), pltpu.VMEM((PARTS, LINE, 8, PART), F32), pltpu.VMEM((PARTS, LINE, 8, PART), F32),
         pltpu.VMEM((16, lru), F32), pltpu.VMEM((2 * lru, rows), BF16), pltpu.VMEM((rows, 2 * lru), BF16), pltpu.VMEM((cols, lru), BF16),
         pltpu.VMEM((2, 16, lru), F32), pltpu.VMEM((2, 2) + retain_weight.shape, F32), pltpu.VMEM((2, 2 * lru, lru), BF16),
         pltpu.VMEM((2, 2 * lru, lru), BF16), by_part(width), by_part(width),
         by_part(width), tok(block, BF16), tok(block), one(block), one(chan, BF16),
         one(chan, F32, 128), one(chan, F32, 128), one(max(5 * chan, 3 * hid)), one(chan, BF16), one(chan, BF16),
         own_low, held, held, held, pltpu.VMEM((2 * hid, width), BF16), pltpu.VMEM((width, 2 * hid), BF16),
         pltpu.VMEM((hid, width), BF16), pltpu.VMEM((width, hid), BF16), one(hid, BF16), one(2 * hid, BF16),
         DMA((5,)), DMA((5,)), DMA((5,)), DMA((PARTS,)), DMA((PARTS,)), DMA((PARTS,))] + line + [DMA((PARTS, 3)), DMA((PARTS, 3))] * 2 + steps * 3 + sums * 3
        + [DMA((7, 7)), DMA((7, 7)), DMA((7,)), DMA((7,)), DMA((7,)), DMA((4,)), DMA((4,)), DMA((4,))],
        0, "forward", 50 * 10**9,
    )(inputs, cotangent, segments[None, :], kernel, offsets[None, :], retain_bias[None, :], admit_bias[None, :],
      lambdas[None, :], mix_gain[None, :], feed_gain[None, :], retain_weight, admit_weight, branch_weight, recur_weight,
      merge_weight, gu_s, down_weight)

    late = seq // LATE
    pair = lambda lead=0: pltpu.VMEM((2, chan, lead + LATE), F32)
    one = lambda n, kind=F32, lead=0: pltpu.VMEM((n, lead + LATE), kind)
    steps = [DMA((2, 3, late)), DMA((2, 3, late))]
    sums = [DMA((2, late, LINE)), DMA((2, late, LINE))]
    held = pltpu.VMEM((late, LINE + 1, block, LATE), BF16)
    own_low = pltpu.VMEM((late, LINE, block, LATE), BF16)
    land = lambda n, m: ((shape((n, m), BF16), ANY), (shape((3, n, m), BF16), ANY))
    input_grad, tiny_v, tiny_g, *sums_of = call(
        functools.partial(back_kernel, width),
        [VM] + [ANY] * 2 + [VM] * 8 + [ANY] * 14,
        [(shape((half, tokens), F32), ANY), (shape((2, 8, chan), F32), VM),
         (shape((lru, 128), F32), VM), *land(cols, 2 * ff), *land(ff, cols), *land(cols, 2 * lru), *land(lru, cols)],
        [pltpu.VMEM((late, LINE, 8, LATE), F32), pltpu.VMEM((8, seq), F32),
         pltpu.VMEM((chan, width), BF16), pltpu.VMEM((width, 2 * chan), BF16),
         pair(), pair(128), pair(), pair(), pair(), pair(128), pltpu.VMEM((late, width, LATE), BF16), tok(2 * chan, BF16),
         tok(block), tok(block), one(chan), one(chan, F32, 128), one(2 * chan, BF16),
         one(chan), one(chan), pltpu.VMEM((chan, 128), F32), own_low, held,
         tok(chan, BF16), by_part(width), pltpu.VMEM((4, cols, 2 * ff), BF16), pltpu.VMEM((cols, 2 * ff), BF16),
         pltpu.VMEM((4, ff, cols), BF16), pltpu.VMEM((ff, cols), BF16),
         pltpu.VMEM((block, 128), F32), pltpu.VMEM((block, 128), F32), pltpu.VMEM((8, chan, 128), F32),
         pltpu.VMEM((2, lru, 2 * lru), F32), by_part(block), pltpu.VMEM((width, 2 * lru), BF16),
         pltpu.VMEM((lru, width), BF16), pltpu.VMEM((2, 8, chan), F32), pltpu.VMEM((2, 8, chan), F32),
         pltpu.VMEM((4, 2, 8, chan), F32), pltpu.VMEM((2, lru, 128), F32), pltpu.VMEM((lru, 128), F32),
         pltpu.VMEM((4, lru, 128), F32), DMA((7,)), DMA((6, 2))] + [DMA((late, 3)), DMA((late, 3))] + steps + sums
        + [DMA, DMA, DMA((2, 2)), DMA((2, LINE)), DMA((2, LINE)), DMA((2,)), DMA((2,)), DMA((4,))]
        + [DMA((2, 3)), DMA((2, 3)), DMA((2, 3)), DMA((2, 3)), DMA((2,)), DMA((2,))],
        2, "mix_backward", 10 * 10**9,
    )(y, dn2, g, x_own, scale_two, scale_one, coef, gains, masks, par, gates, m_n, br_n, b, p, u, r, i, h,
      q, n1, f_own, f_got, fd_own, fd_got)

    line_of = shape((1, lru), F32)
    cuts = 3
    rows_in = lambda *dims: pl.BlockSpec((dims[0] // cuts,) + dims[1:], lambda n: (n,) + (0,) * (len(dims) - 1))
    three = lambda *dims: pl.BlockSpec((3, dims[0] // cuts, dims[1]), lambda n: (0, n, 0))
    still = lambda *dims: pl.BlockSpec(dims, lambda n: (0,) * len(dims))
    sizes = ((cols, 2 * ff), (ff, cols), (cols, 2 * lru), (lru, cols))
    big = ((cols, lru), (cols, lru), (lru, cols), (ff, cols), (ff, cols), (ff, cols))
    across = pl.BlockSpec((ff, cols // cuts), lambda n: (0, n))
    flat = ((4, lru),) + ((1, lru),) * 4 + ((1, half),) * 2 + ((heads, 64, 64),) * 2
    s_b, s_r, s_m, s_g, s_u, s_d, result, input_grad, taps, offs, bias_r, bias_a, decay, mix, feed, retain, admit = pl.pallas_call(
        last_kernel,
        grid=(cuts,),
        out_shape=[shape(d, F32) for d in big] + [shape((half, tokens), BF16), shape((half, tokens), F32)]
        + [shape(d, F32) for d in flat],
        in_specs=[spec(*d) for d in sizes[:3] for spec in (rows_in, three)] + [still(lru, cols), still(3, lru, cols)]
        + [rows_in(half, tokens)] * 2
        + [still(2, 8, chan), still(lru, 128), still(1, lru)],
        out_specs=[rows_in(cols, lru)] * 2 + [still(lru, cols)] + [across] * 2 + [rows_in(ff, cols)] + [rows_in(half, tokens)] * 2 + [still(*d) for d in flat],
        name="last_sums",
        compiler_params=pltpu.CompilerParams(vmem_limit_bytes=ROOM),
    )(*sums_of, result, input_grad, tiny_v, tiny_g, lambdas[None, :])
    return (
        result,
        input_grad,
        mix[0],
        s_b,
        s_r,
        taps,
        offs[0],
        retain,
        bias_r[0],
        admit,
        bias_a[0],
        decay[0],
        s_m,
        feed[0],
        s_g.T,
        s_u.T,
        s_d,
    )


def suits(mesh, args):
    return (
        dict(mesh.shape) == {"row": 4, "col": 8}
        and args[0].shape == (D, 8 * SEQ)
        and args[3].shape == (D, 2048)
        and args[14].shape == (D, 4608)
        and args[7].shape == (32, 64, 64)
    )


def solution(mesh):
    in_specs = (
        P("col", "row"),
        P("row"),
        P("col"),
        P("row", "col"),
        P("row", "col"),
        P(None, "col"),
        P("col"),
        P("col", None, None),
        P("col"),
        P("col", None, None),
        P("col"),
        P("col"),
        P("col", "row"),
        P("col"),
        P("row", "col"),
        P("row", "col"),
        P("col", "row"),
        P("col", "row"),
    )
    out_specs = (
        P("col", "row"),
        P("col", "row"),
        P("col"),
        P("row", "col"),
        P("row", "col"),
        P(None, "col"),
        P("col"),
        P("col", None, None),
        P("col"),
        P("col", None, None),
        P("col"),
        P("col"),
        P("col", "row"),
        P("col"),
        P("row", "col"),
        P("row", "col"),
        P("col", "row"),
    )
    def run(*args):
        chosen = fast_body if suits(mesh, args) else body
        return jax.shard_map(
            chosen, mesh=mesh, in_specs=in_specs, out_specs=out_specs, check_vma=False
        )(*args)

    return run
```

profile of v0, /device:TPU:0, one launch (start us, length us, event | category | flops | bytes accessed | tf_op | source)
XLA Modules:
  0.0 433.6 jit_solution(9091897054590458998)
XLA Ops:
  0.7 2.1 maximum_bitcast_fusion.gu_s
  2.8 293.6 %forward.1 = (f32[8,1152]{1,0:T(8,128)}, f32[512,16]{1,0:T(8,128)}, f32[384,16]{1,0:T(8,128)}, bf16[2,256,512]{2,1,0:T(8,128)(2,1)}, f32[8,1024]{1,0:T(8,128)}, ...) custom-call(bf16[192,2048]{1,0:T(8,128)(2,1)} %x_in.1, ...), custom_call_target="tpu_custom_call" | custom-call | flops 49999998976 | bytes 40000000 | tf_op jit(solution)/shard_map/forward/pallas_call | solution.py:1641
  296.4 129.0 %mix_backward.1 = (f32[192,2048]{1,0:T(8,128)}, f32[2,8,512]{2,1,0:T(8,128)}, f32[256,128]{1,0:T(8,128)}, bf16[384,1152]{1,0:T(8,128)(2,1)}, bf16[3,384,1152]{2,...) custom-call(f32[384,1024]{1,0:T(8,128)} %get-tuple-element.71.y, ...), custom_call_target="tpu_custom_call" | custom-call | flops 10000000000 | bytes 40000000 | tf_op jit(solution)/shard_map/mix_backward/pallas_call | solution.py:1671
  425.4 8.0 %last_sums.1 = (f32[384,256]{1,0:T(8,128)}, f32[384,256]{1,0:T(8,128)}, f32[256,384]{1,0:T(8,128)}, f32[576,384]{1,0:T(8,128)}, f32[576,384]{1,0:T(8,128)}, /*in...) custom-call(bf16[384,1152]{1,0:T(8,128)(2,1)} %get-tuple-element.96., ...), custom_call_target="tpu_custom_call" | custom-call | tf_op jit(solution)/shard_map/last_sums/pallas_call | solution.py:1703
where the time goes:
time: 434 us
  Pallas kernels  431 us (99%)
    pallas_call x1, Pallas kernels, fast_body(): call(functools.partial(forward_kernel, width, EPS), [ANY] * 2 + [VM] * 13...  294 us
    pallas_call x1, Pallas kernels, fast_body(): call(functools.partial(back_kernel, width), [VM] + [ANY] * 2 + [VM] * 8 +...  129 us

commit v1 on v0

--- a/solution.py
+++ b/solution.py
@@ -707,7 +707,6 @@
 
     blocks(block // 16, norm)
     gather.send(0, 0)
-    gather.send(0, 1)
     p_s[:, PART:] = jnp.zeros((chan, 128), F32)
     h_s[:, PART:] = jnp.zeros((chan, 128), F32)
     pads = [
@@ -740,17 +739,17 @@
         if lag == 1:
             masks[0:1, 0:seq] = 1.0 - same[0:1]
     gather.forward(1, 0)
-    gather.send(0, 2)
+    gather.send(0, 1)
+    weights[0].forward()
+    gather.forward(2, 0)
     gather_go.forward(1, 0)
     gather.forward(1, 1)
-    gather.forward(2, 0)
-    weights[0].forward()
-    gather_go.forward(1, 1)
-    gather_go.forward(2, 0)
+    gather.send(0, 2)
     weights[1].forward()
     for w in weights[3:5]:
         w.start()
-    gather_go.forward(2, 1)
+    gather_go.forward(1, 1)
+    gather_go.forward(2, 0)
     weights[0].finish()
     for pad in pads:
         pad.wait()
@@ -915,6 +914,7 @@
         keep(n, PARTS - 1).wait()
     flush_n = pltpu.make_async_copy(normed, n1_out, v_sem.at[4])
     flush_n.start()
+    gather_go.forward(2, 1)
     gather_go.send(0, 2)
     gather_go.send(0, 3)
     spread.serve(PARTS, finish)
@@ -937,12 +937,23 @@
     weights[3].finish()
     blocks(2 * hid // 128, turn_up)
     norm_two(PARTS - 1)
+    flush_y = pltpu.make_async_copy(y, y_out, v_sem.at[2])
+    flush_y.start()
 
     def keep_dev(k):
         return pltpu.make_async_copy(dev, dev_h.at[:, lanes(k)], v_sem.at[5])
 
     def keep_z(k):
         return pltpu.make_async_copy(zs, z_h.at[:, lanes(k)], v_sem.at[6])
+
+    dev_all, z_all = gu.at[:, 0:seq], dt.at[0:hid, 0:seq]
+    before, end = pl.ds(0, seq - PART), pl.ds(seq - PART, PART)
+    loads = [
+        pltpu.make_async_copy(dev_h.at[:, before], gu.at[:, before], v_sem.at[7]),
+        pltpu.make_async_copy(z_h.at[:, before], dt.at[0:hid, before], v_sem.at[8]),
+        pltpu.make_async_copy(dev, gu.at[:, end], v_sem.at[9]),
+        pltpu.make_async_copy(zs, dt.at[0:hid, end], v_sem.at[10]),
+    ]
 
     def feed(k):
 
@@ -952,6 +963,12 @@
             keep_z(k - 1).wait()
 
         ev[...] = dot(gu[...], normed2[k])
+
+        @pl.when(k == PARTS - 1)
+        def _():
+            weights[3].sent()
+            loads[0].start()
+
         gather_two.middle(k)
         gather_go.middle(k, 2)
         gather_go.arrive(2, k)
@@ -1017,16 +1034,13 @@
         return carry
 
     lax.fori_loop(0, PARTS, feed_step, 0)
-    for w in weights[3:5]:
-        w.sent()
+    weights[4].sent()
+    for load in loads[1:]:
+        load.start()
     keep_dev(PARTS - 1).wait()
     keep_z(PARTS - 1).wait()
-    dev_all, z_all = gu.at[:, 0:seq], dt.at[0:hid, 0:seq]
-    loads = [pltpu.make_async_copy(dev_h, dev_all, v_sem.at[5]), pltpu.make_async_copy(z_h, z_all, v_sem.at[6])]
-    for load in loads:
-        load.start()
-    for load in loads:
-        load.wait()
+    loads[0].wait()
+    loads[2].wait()
 
     def columns(start):
         return pl.ds(pl.multiple_of(start, 128), block)
@@ -1076,6 +1090,11 @@
         spread_n.serve(t, finish_n)
         spread_o.serve(t, finish_o)
 
+        @pl.when(i == 0)
+        def _():
+            loads[1].wait()
+            loads[3].wait()
+
         @pl.when(i < 2)
         def _():
             grad_down(jnp.where(i == 0, 1 - core, core))
@@ -1088,10 +1107,10 @@
     last = [
         remote(res.at[rows_of(1 - core, half), :], result.at[:, mine], x_send.at[0], x_recv.at[0], sibling),
         pltpu.make_async_copy(res.at[rows_of(core, half), :], result.at[:, mine], x_loc.at[0]),
-        pltpu.make_async_copy(y, y_out, v_sem.at[2]),
         keep_n(PARTS - 1),
+        flush_y,
     ]
-    for copy in last[:3]:
+    for copy in last[:2]:
         copy.start()
     for w in weights[5:]:
         w.finish()
@@ -1197,15 +1216,13 @@
     outer(PARTS - 1)
     met()
     gather.send(0, 0)
-    outer(PARTS - 2)
+    for part in range(PARTS - 2, -1, -1):
+        outer(part)
+    gather.forward(1, 0)
     gather.send(0, 1)
-    outer(PARTS - 3)
-    gather.forward(1, 0)
+    gather.forward(2, 0)
+    gather.forward(1, 1)
     gather.send(0, 2)
-    for part in range(PARTS - 3):
-        outer(part)
-    gather.forward(1, 1)
-    gather.forward(2, 0)
     spread = Spread(lambda k, s: own.at[k, s], held, s_send, s_recv, z, core)
     load_m.wait()
     load_b.wait()
@@ -1458,18 +1475,24 @@
             for d in (3, 2, 1, 0):
                 out_br(d).start()
         spread.serve(t, finish)
+        pl.when(i == 0)(tiny_open)
+        pl.when(i == 1)(tiny_more)
         return carry
 
-    lax.fori_loop(0, LINE - 1, drain, 0)
     mine = pl.ds(pl.multiple_of(core * seq, seq), seq)
-    for side in (0, 1):
-        for e in range(4):
-            at = slice(e * 64, (e + 1) * 64)
-            gd[side, at, 0:64] = gate_grad[side, at, e * 64 : (e + 1) * 64]
-            gd[side, at, 64:128] = gate_grad[side, at, 256 + e * 64 : 256 + (e + 1) * 64]
+    lane = lax.broadcasted_iota(jnp.int32, (64, 128), 1)
     swap_gd = remote(gd.at[1 - core], gd_in, v_send.at[0], v_recv.at[0], sibling)
-    swap_gd.start()
-    lane = lax.broadcasted_iota(jnp.int32, (64, 128), 1)
+    rows_gd = [
+        remote(gd_all.at[0], gd_all.at[d], n_send.at[0, d - 1], n_recv.at[0, d - 1], {"row": row ^ d}) for d in (1, 2, 3)
+    ]
+
+    def tiny_open():
+        for side in (0, 1):
+            for e in range(4):
+                at = slice(e * 64, (e + 1) * 64)
+                gd[side, at, 0:64] = gate_grad[side, at, e * 64 : (e + 1) * 64]
+                gd[side, at, 64:128] = gate_grad[side, at, 256 + e * 64 : 256 + (e + 1) * 64]
+        swap_gd.start()
 
     def columns(parts, at):
         total = jnp.zeros((64, 128), F32)
@@ -1477,12 +1500,24 @@
             total = total + jnp.where(lane == n, jnp.sum(part(at), axis=1, keepdims=True), 0.0)
         return total
 
-    vec[...] = jnp.zeros(vec.shape, F32)
-    for j in range(chan // 64):
+    def tiny_more():
+        swap_gd.wait()
+        gd_all[0] = gd[core] + gd_in[...]
+        for copy in rows_gd:
+            copy.start()
+        vec[...] = jnp.zeros(vec.shape, F32)
+        for j in range(chan // 64):
+            at = slice(j * 64, (j + 1) * 64)
+            v = columns([lambda at, n=n: small[n, at, :] for n in range(8)], at)
+            vec[0, :, at] = v.T[0:8, :]
+
+    lax.fori_loop(0, LINE - 1, drain, 0)
+    for j in range(block // 64):
         at = slice(j * 64, (j + 1) * 64)
-        v = columns([lambda at, n=n: small[n, at, :] for n in range(8)], at)
-        vec[0, :, at] = v.T[0:8, :]
-
+        v = columns([lambda at: mix_part[at, :], lambda at: feed_part[at, :]], at)
+        vec[1, :, at] = v.T[0:8, :]
+    swap_vec = remote(vec, vec_in, v_send.at[1], v_recv.at[1], sibling)
+    swap_vec.start()
     for k in range(PARTS):
         for d in (1, 2, 3):
             share(k, d).wait_send()
@@ -1505,19 +1540,6 @@
     back.start()
     keep_in = pltpu.make_async_copy(dy.at[rows_of(core, half), :], input_grad.at[:, mine], d_own.at[3])
     keep_in.start()
-    for j in range(block // 64):
-        at = slice(j * 64, (j + 1) * 64)
-        v = columns([lambda at: mix_part[at, :], lambda at: feed_part[at, :]], at)
-        vec[1, :, at] = v.T[0:8, :]
-    swap_vec = remote(vec, vec_in, v_send.at[1], v_recv.at[1], sibling)
-    swap_vec.start()
-    swap_gd.wait()
-    gd_all[0] = gd[core] + gd_in[...]
-    rows_gd = [
-        remote(gd_all.at[0], gd_all.at[d], n_send.at[0, d - 1], n_recv.at[0, d - 1], {"row": row ^ d}) for d in (1, 2, 3)
-    ]
-    for copy in rows_gd:
-        copy.start()
     swap_vec.wait()
     vec_all[0] = vec[...] + vec_in[...]
     rows_vec = [
@@ -1654,7 +1676,7 @@
          own_low, held, held, held, pltpu.VMEM((2 * hid, width), BF16), pltpu.VMEM((width, 2 * hid), BF16),
          pltpu.VMEM((hid, width), BF16), pltpu.VMEM((width, hid), BF16), one(hid, BF16), one(2 * hid, BF16),
          DMA((5,)), DMA((5,)), DMA((5,)), DMA((PARTS,)), DMA((PARTS,)), DMA((PARTS,))] + line + [DMA((PARTS, 3)), DMA((PARTS, 3))] * 2 + steps * 3 + sums * 3
-        + [DMA((7, 7)), DMA((7, 7)), DMA((7,)), DMA((7,)), DMA((7,)), DMA((4,)), DMA((4,)), DMA((4,))],
+        + [DMA((7, 7)), DMA((7, 7)), DMA((7,)), DMA((7,)), DMA((11,)), DMA((4,)), DMA((4,)), DMA((4,))],
         0, "forward", 50 * 10**9,
     )(inputs, cotangent, segments[None, :], kernel, offsets[None, :], retain_bias[None, :], admit_bias[None, :],
       lambdas[None, :], mix_gain[None, :], feed_gain[None, :], retain_weight, admit_weight, branch_weight, recur_weight,

time: 434 us -> 430 us (level)
  no operation moved by 1% of the time
where the time goes in v1:
time: 430 us
  Pallas kernels  427 us (99%)
    pallas_call x1, Pallas kernels, fast_body(): call(functools.partial(forward_kernel, width, EPS), [ANY] * 2 + [VM] * 13...  291 us
    pallas_call x1, Pallas kernels, fast_body(): call(functools.partial(back_kernel, width), [VM] + [ANY] * 2 + [VM] * 8 +...  127 us

profile of v1, /device:TPU:0, one launch (start us, length us, event | category | flops | bytes accessed | tf_op | source)
XLA Modules:
  0.0 429.6 jit_solution(1228100773216794853)
XLA Ops:
  0.7 2.1 maximum_bitcast_fusion.gu_s
  2.8 291.4 %forward.1 = (f32[8,1152]{1,0:T(8,128)}, f32[512,16]{1,0:T(8,128)}, f32[384,16]{1,0:T(8,128)}, bf16[2,256,512]{2,1,0:T(8,128)(2,1)}, f32[8,1024]{1,0:T(8,128)}, ...) custom-call(bf16[192,2048]{1,0:T(8,128)(2,1)} %x_in.1, ...), custom_call_target="tpu_custom_call" | custom-call | flops 49999998976 | bytes 40000000 | tf_op jit(solution)/shard_map/forward/pallas_call | solution.py:1663
  294.2 127.2 %mix_backward.1 = (f32[192,2048]{1,0:T(8,128)}, f32[2,8,512]{2,1,0:T(8,128)}, f32[256,128]{1,0:T(8,128)}, bf16[384,1152]{1,0:T(8,128)(2,1)}, bf16[3,384,1152]{2,...) custom-call(f32[384,1024]{1,0:T(8,128)} %get-tuple-element.71.y, ...), custom_call_target="tpu_custom_call" | custom-call | flops 10000000000 | bytes 40000000 | tf_op jit(solution)/shard_map/mix_backward/pallas_call | solution.py:1693
  421.4 8.0 %last_sums.1 = (f32[384,256]{1,0:T(8,128)}, f32[384,256]{1,0:T(8,128)}, f32[256,384]{1,0:T(8,128)}, f32[576,384]{1,0:T(8,128)}, f32[576,384]{1,0:T(8,128)}, /*in...) custom-call(bf16[384,1152]{1,0:T(8,128)(2,1)} %get-tuple-element.96., ...), custom_call_target="tpu_custom_call" | custom-call | tf_op jit(solution)/shard_map/last_sums/pallas_call | solution.py:1725

commit v2 on v1

--- a/solution.py
+++ b/solution.py
@@ -921,6 +921,8 @@
     square(PARTS - 3)
     norm_two(PARTS - 4)
     gather_two.forward(2, 0)
+    weights[3].finish()
+    blocks(2 * hid // 128, turn_up)
     weights[4].forward()
     spread.serve(PARTS + 1, finish)
     square(PARTS - 2)
@@ -928,17 +930,10 @@
     gather_go.forward(1, 2)
     weights[4].finish()
     blocks(hid // 128, turn_down)
-    spread.serve(PARTS + 2, finish)
-    square(PARTS - 1)
-    norm_two(PARTS - 2)
     gather.sent()
     for flush in flushes + [flush_n]:
         flush.wait()
-    weights[3].finish()
-    blocks(2 * hid // 128, turn_up)
-    norm_two(PARTS - 1)
     flush_y = pltpu.make_async_copy(y, y_out, v_sem.at[2])
-    flush_y.start()
 
     def keep_dev(k):
         return pltpu.make_async_copy(dev, dev_h.at[:, lanes(k)], v_sem.at[5])
@@ -992,6 +987,17 @@
         spread_o.serve(k, finish_o)
         keep_dev(k).start()
         keep_z(k).start()
+
+        @pl.when(k == 0)
+        def _():
+            spread.serve(PARTS + 2, finish)
+            square(PARTS - 1)
+            norm_two(PARTS - 2)
+
+        @pl.when(k == 1)
+        def _():
+            norm_two(PARTS - 1)
+            flush_y.start()
 
     def finish_o(k, total):
         def add(i):

time: 430 us -> 426 us (level)
  Pallas kernels: 427 us -> 422 us
where the time goes in v2:
time: 426 us; the launch traced here: 425 us
  Pallas kernels  422 us (99%)
    pallas_call x1, Pallas kernels, fast_body(): call(functools.partial(forward_kernel, width, EPS), [ANY] * 2 + [VM] * 13...  287 us
    pallas_call x1, Pallas kernels, fast_body(): call(functools.partial(back_kernel, width), [VM] + [ANY] * 2 + [VM] * 8 +...  127 us

profile of v2, /device:TPU:0, one launch (start us, length us, event | category | flops | bytes accessed | tf_op | source)
XLA Modules:
  0.0 425.4 jit_solution(5719455982673556863)
XLA Ops:
  0.7 2.1 maximum_bitcast_fusion.gu_s
  2.8 287.2 %forward.1 = (f32[8,1152]{1,0:T(8,128)}, f32[512,16]{1,0:T(8,128)}, f32[384,16]{1,0:T(8,128)}, bf16[2,256,512]{2,1,0:T(8,128)(2,1)}, f32[8,1024]{1,0:T(8,128)}, ...) custom-call(bf16[192,2048]{1,0:T(8,128)(2,1)} %x_in.1, ...), custom_call_target="tpu_custom_call" | custom-call | flops 49999998976 | bytes 40000000 | tf_op jit(solution)/shard_map/forward/pallas_call | solution.py:1669
  290.0 127.2 %mix_backward.1 = (f32[192,2048]{1,0:T(8,128)}, f32[2,8,512]{2,1,0:T(8,128)}, f32[256,128]{1,0:T(8,128)}, bf16[384,1152]{1,0:T(8,128)(2,1)}, bf16[3,384,1152]{2,...) custom-call(f32[384,1024]{1,0:T(8,128)} %get-tuple-element.71.y, ...), custom_call_target="tpu_custom_call" | custom-call | flops 10000000000 | bytes 40000000 | tf_op jit(solution)/shard_map/mix_backward/pallas_call | solution.py:1699
  417.2 8.0 %last_sums.1 = (f32[384,256]{1,0:T(8,128)}, f32[384,256]{1,0:T(8,128)}, f32[256,384]{1,0:T(8,128)}, f32[576,384]{1,0:T(8,128)}, f32[576,384]{1,0:T(8,128)}, /*in...) custom-call(bf16[384,1152]{1,0:T(8,128)(2,1)} %get-tuple-element.96., ...), custom_call_target="tpu_custom_call" | custom-call | tf_op jit(solution)/shard_map/last_sums/pallas_call | solution.py:1731

commit v3 on v2

--- a/solution.py
+++ b/solution.py
@@ -1092,9 +1092,10 @@
 
     def drain(i, carry):
         t = PARTS + i
-        blocks(2, lambda j: grad_up(2 * i + j))
+        grad_up(2 * i)
         spread_n.serve(t, finish_n)
         spread_o.serve(t, finish_o)
+        grad_up(2 * i + 1)
 
         @pl.when(i == 0)
         def _():

time: 426 us -> 430 us (level)
  no operation moved by 1% of the time
where the time goes in v3:
time: 430 us; the launch traced here: 429 us
  Pallas kernels  426 us (99%)
    pallas_call x1, Pallas kernels, fast_body(): call(functools.partial(forward_kernel, width, EPS), [ANY] * 2 + [VM] * 13...  287 us
    pallas_call x1, Pallas kernels, fast_body(): call(functools.partial(back_kernel, width), [VM] + [ANY] * 2 + [VM] * 8 +...  131 us

profile of v3, /device:TPU:0, one launch (start us, length us, event | category | flops | bytes accessed | tf_op | source)
XLA Modules:
  0.0 429.4 jit_solution(4333951715227414781)
XLA Ops:
  0.7 2.1 maximum_bitcast_fusion.gu_s
  2.8 287.3 %forward.1 = (f32[8,1152]{1,0:T(8,128)}, f32[512,16]{1,0:T(8,128)}, f32[384,16]{1,0:T(8,128)}, bf16[2,256,512]{2,1,0:T(8,128)(2,1)}, f32[8,1024]{1,0:T(8,128)}, ...) custom-call(bf16[192,2048]{1,0:T(8,128)(2,1)} %x_in.1, ...), custom_call_target="tpu_custom_call" | custom-call | flops 49999998976 | bytes 40000000 | tf_op jit(solution)/shard_map/forward/pallas_call | solution.py:1670
  290.1 131.1 %mix_backward.1 = (f32[192,2048]{1,0:T(8,128)}, f32[2,8,512]{2,1,0:T(8,128)}, f32[256,128]{1,0:T(8,128)}, bf16[384,1152]{1,0:T(8,128)(2,1)}, bf16[3,384,1152]{2,...) custom-call(f32[384,1024]{1,0:T(8,128)} %get-tuple-element.71.y, ...), custom_call_target="tpu_custom_call" | custom-call | flops 10000000000 | bytes 40000000 | tf_op jit(solution)/shard_map/mix_backward/pallas_call | solution.py:1700
  421.2 8.0 %last_sums.1 = (f32[384,256]{1,0:T(8,128)}, f32[384,256]{1,0:T(8,128)}, f32[256,384]{1,0:T(8,128)}, f32[576,384]{1,0:T(8,128)}, f32[576,384]{1,0:T(8,128)}, /*in...) custom-call(bf16[384,1152]{1,0:T(8,128)(2,1)} %get-tuple-element.96., ...), custom_call_target="tpu_custom_call" | custom-call | tf_op jit(solution)/shard_map/last_sums/pallas_call | solution.py:1732

commit v4 on v2

--- a/solution.py
+++ b/solution.py
@@ -775,6 +775,7 @@
             for n in range(len(kept)):
                 keep(n, k - 1).wait()
 
+        gather.middle(k)
         p_s[:, 0:128] = p_s[:, PART:]
         h_s[:, 0:128] = h_s[:, PART:]
         p_s[:, 128:] = dot(br[0:chan, :], normed[k])
@@ -792,7 +793,6 @@
             ul[ch, :] = (u - high.astype(F32)).astype(BF16)
 
         blocks(chan // 64, conv)
-        gather.middle(k)
         for g in range(chan // 256):
             at = slice(g * 256, (g + 1) * 256)
             pre = dot(gates_hi[g], uh[at, :]) + dot(gates_hi[g], ul[at, :]) + dot(gates_lo[g], uh[at, :])
@@ -957,6 +957,8 @@
             keep_dev(k - 1).wait()
             keep_z(k - 1).wait()
 
+        gather_two.middle(k)
+        gather_go.middle(k, 2)
         ev[...] = dot(gu[...], normed2[k])
 
         @pl.when(k == PARTS - 1)
@@ -964,8 +966,6 @@
             weights[3].sent()
             loads[0].start()
 
-        gather_two.middle(k)
-        gather_go.middle(k, 2)
         gather_go.arrive(2, k)
         dz[...] = dot(down[...], go[k])
         for c in range(2):
@@ -1298,6 +1298,7 @@
         def _():
             fetch_all(k - 1)
 
+        gather.middle(t)
         dq[...] = dot(m_n[...], dyf[k])
 
         @pl.when(t == PARTS - 1)
@@ -1320,7 +1321,6 @@
             a_c[ch, :] = jnp.exp(-(r_s[slot, ch, :] * pr[:, 7:8]))
 
         blocks(chan // 64, before)
-        gather.middle(t)
 
         def recur(i):
             ch = rows_of(i, 128)

time: 426 us -> 433 us (1.016)
  Pallas kernels: 422 us -> 429 us
    pallas_call x1, Pallas kernels: 287 us -> 293 us  [fast_body(): call(functools.partial(forward_kernel, width, EPS), [ANY] * 2 + [VM] * 13...]
where the time goes in v4:
time: 433 us; the launch traced here: 432 us
  Pallas kernels  429 us (99%)
    pallas_call x1, Pallas kernels, fast_body(): call(functools.partial(forward_kernel, width, EPS), [ANY] * 2 + [VM] * 13...  293 us
    pallas_call x1, Pallas kernels, fast_body(): call(functools.partial(back_kernel, width), [VM] + [ANY] * 2 + [VM] * 8 +...  128 us

profile of v4, /device:TPU:0, one launch (start us, length us, event | category | flops | bytes accessed | tf_op | source)
XLA Modules:
  0.0 432.4 jit_solution(5565215841085033893)
XLA Ops:
  0.7 2.1 maximum_bitcast_fusion.gu_s
  2.8 293.2 %forward.1 = (f32[8,1152]{1,0:T(8,128)}, f32[512,16]{1,0:T(8,128)}, f32[384,16]{1,0:T(8,128)}, bf16[2,256,512]{2,1,0:T(8,128)(2,1)}, f32[8,1024]{1,0:T(8,128)}, ...) custom-call(bf16[192,2048]{1,0:T(8,128)(2,1)} %x_in.1, ...), custom_call_target="tpu_custom_call" | custom-call | flops 49999998976 | bytes 40000000 | tf_op jit(solution)/shard_map/forward/pallas_call | solution.py:1669
  296.0 128.2 %mix_backward.1 = (f32[192,2048]{1,0:T(8,128)}, f32[2,8,512]{2,1,0:T(8,128)}, f32[256,128]{1,0:T(8,128)}, bf16[384,1152]{1,0:T(8,128)(2,1)}, bf16[3,384,1152]{2,...) custom-call(f32[384,1024]{1,0:T(8,128)} %get-tuple-element.71.y, ...), custom_call_target="tpu_custom_call" | custom-call | flops 10000000000 | bytes 40000000 | tf_op jit(solution)/shard_map/mix_backward/pallas_call | solution.py:1699
  424.2 8.0 %last_sums.1 = (f32[384,256]{1,0:T(8,128)}, f32[384,256]{1,0:T(8,128)}, f32[256,384]{1,0:T(8,128)}, f32[576,384]{1,0:T(8,128)}, f32[576,384]{1,0:T(8,128)}, /*in...) custom-call(bf16[384,1152]{1,0:T(8,128)(2,1)} %get-tuple-element.96., ...), custom_call_target="tpu_custom_call" | custom-call | tf_op jit(solution)/shard_map/last_sums/pallas_call | solution.py:1731
